TPU v7x, 256 devices: a whole 4x4x8 slice. The times are simulated.
256 devices in a mesh: ctx: 32 (over z, y_lo, core), grp: 8 (over x, y_hi).
Axes of the slice: x: 4, y: 4 (y_hi: 2, y_lo: 2; y = y_hi * 2 + y_lo), z: 8, core: 2. Of those that a mesh axis runs over, the one named last changes fastest.
Arguments:
- queries: bfloat16 [8, 4096, 1792], P('grp', 'ctx'), may hold values from -160 to 160
- keys: bfloat16 [8, 4096, 256], P('grp', 'ctx'), may hold values from -6 to 6
- values: bfloat16 [8, 4096, 256], P('grp', 'ctx'), may hold values from -6 to 6
- segment_ids: int32 [8, 4096], P('grp', 'ctx'), may hold values from 0 to 3, never falling along the last dimension, each value on 1 to 3072 neighbouring positions
- turn_start: int32 [8, 32], P('grp'), may hold values from 0 to 4095, as said below
- turn_len: int32 [8, 32], P('grp'), may hold values from 1 to 40, as said below
- w_proj: bfloat16 [1792, 896], replicated, may hold values from -0.125 to 0.125
- gain: float32 [896], replicated, may hold values from 0.1 to 1.9
- gate_w: bfloat16 [9472, 896], P('ctx'), may hold values from -0.1875 to 0.1875
- up_w: bfloat16 [9472, 896], P('ctx'), may hold values from -0.1875 to 0.1875
- down_w: bfloat16 [9472, 896], P('ctx'), may hold values from -0.0625 to 0.0625
- cotangent: bfloat16 [8, 4096, 896], P('grp', 'ctx'), may hold values from -0.1875 to 0.1875
Outputs:
- context: bfloat16 [8, 4096, 1792], P('grp', 'ctx')
- talker_out: bfloat16 [8, 4096, 896], P('grp', 'ctx')
- grad_gate: float32 [9472, 896], P('ctx')
- grad_up: float32 [9472, 896], P('ctx')
- grad_down: float32 [9472, 896], P('ctx')
Inputs may be any that keep to these rules, and one draw needn't show every extreme that they name: `turn_start`: turn t of a dialogue lies inside positions t * 128 to (t + 1) * 128 - 1, so turns don't intersect. `turn_len`: every dialogue has a turn of exactly 40 positions.
All inputs are finite; a program needn't handle non-finite values.
Results may differ from a plain program's by a relative error of at most 0.03.
Values may be sent and summed in bfloat16 or wider, within the bound.
A program may use at most 128 MiB of HBM per device.

v0:
```python
import math

import jax
import jax.numpy as jnp
from jax import lax
from jax.sharding import PartitionSpec as P

HEADS = 14
KV_HEADS = 2
HEAD_DIM = 128
ASSIST_DEV = 40


def collect_cot(packer, cot_block):
    own_cot = jnp.dot(packer, cot_block, preferred_element_type=jnp.float32).astype(jnp.bfloat16)
    return lax.all_gather(own_cot, "ctx", axis=0, tiled=True)


def shards(
    queries,
    keys,
    values,
    segment_ids,
    turn_start,
    turn_len,
    w_proj,
    gain,
    gate_w,
    up_w,
    down_w,
    cotangent,
):
    query_rows = queries[0]
    tok_count = query_rows.shape[0]
    group_size = HEADS // KV_HEADS
    att_scale = 1.0 / math.sqrt(HEAD_DIM)
    ctx_index = lax.axis_index("ctx")
    query_pos = ctx_index * tok_count + jnp.arange(tok_count, dtype=jnp.int32)
    query_heads = query_rows.reshape(tok_count, KV_HEADS, group_size, HEAD_DIM)
    segment_wire = segment_ids[0].astype(jnp.bfloat16)
    turn_end = turn_start[0] + turn_len[0]
    assistant = jnp.any(
        (query_pos[:, None] >= turn_start[0][None, :]) & (query_pos[:, None] < turn_end[None, :]),
        axis=1,
    )
    slots = jnp.cumsum(assistant.astype(jnp.int32)) - 1
    slot_count = ASSIST_DEV
    slot_ids = jnp.arange(slot_count, dtype=jnp.int32)
    packer = ((slots[None, :] == slot_ids[:, None]) & assistant[None, :]).astype(jnp.bfloat16)
    key_piece = lax.all_gather(keys[0], "ctx", axis=0, tiled=True)
    value_piece = lax.all_gather(values[0], "ctx", axis=0, tiled=True)
    seg_piece = lax.all_gather(segment_wire, "ctx", axis=0, tiled=True)
    piece_len = key_piece.shape[0]
    key_pos = jnp.arange(piece_len, dtype=jnp.int32)
    allowed = (key_pos[None, :] <= query_pos[:, None]) & (
        seg_piece[None, :] == segment_wire[:, None]
    )
    allowed_wide = allowed[:, None, None, :]
    row_max = jnp.full((tok_count, KV_HEADS, group_size), -1e30, jnp.float32)
    scores = (
        jnp.einsum(
            "tkgd,skd->tkgs",
            query_heads,
            key_piece.reshape(piece_len, KV_HEADS, HEAD_DIM),
            preferred_element_type=jnp.float32,
        )
        * att_scale
    )
    scores = jnp.where(allowed_wide, scores, -1e30)
    new_max = jnp.maximum(row_max, jnp.max(scores, axis=-1))
    probs = jnp.where(allowed_wide, jnp.exp(scores - new_max[..., None]), 0.0)
    new_sum = jnp.sum(probs, axis=-1)
    update_out = jnp.einsum(
        "tkgs,skd->tkgd",
        probs.astype(jnp.bfloat16),
        value_piece.reshape(piece_len, KV_HEADS, HEAD_DIM),
        preferred_element_type=jnp.float32,
    )
    context = (
        (update_out / new_sum[..., None]).reshape(tok_count, HEADS * HEAD_DIM).astype(jnp.bfloat16)
    )
    talker_in = jnp.dot(context, w_proj, preferred_element_type=jnp.float32).astype(jnp.bfloat16)
    own_rows = jnp.dot(packer, talker_in, preferred_element_type=jnp.float32)
    normed = (
        own_rows * lax.rsqrt(jnp.mean(own_rows * own_rows, axis=-1, keepdims=True) + 1e-06) * gain
    ).astype(jnp.bfloat16)
    rows_all = lax.all_gather(normed, "ctx", axis=0, tiled=True)
    contract_last = (((1,), (1,)), ((), ()))
    contract_first = (((0,), (0,)), ((), ()))
    gate_pre = lax.dot_general(gate_w, rows_all, contract_last, preferred_element_type=jnp.float32)
    up_pre = lax.dot_general(up_w, rows_all, contract_last, preferred_element_type=jnp.float32)
    sigmoid_gate = jax.nn.sigmoid(gate_pre)
    activated = gate_pre * sigmoid_gate
    hidden_t = (activated * up_pre).astype(jnp.bfloat16)
    ffn_rows = lax.psum_scatter(
        lax.dot_general(
            hidden_t, down_w, contract_first, preferred_element_type=jnp.float32
        ).astype(jnp.bfloat16),
        "ctx",
        scatter_dimension=0,
        tiled=True,
    ).astype(jnp.float32)
    out_rows = (own_rows + ffn_rows).astype(jnp.bfloat16)
    talker_out = lax.dot_general(
        packer, out_rows, contract_first, preferred_element_type=jnp.float32
    ).astype(jnp.bfloat16)
    cot_all = collect_cot(packer, cotangent[0])
    d_hidden = lax.dot_general(down_w, cot_all, contract_last, preferred_element_type=jnp.float32)
    grad_down = jnp.dot(hidden_t, cot_all, preferred_element_type=jnp.float32)
    d_gate = (d_hidden * up_pre * sigmoid_gate * (1.0 + gate_pre * (1.0 - sigmoid_gate))).astype(
        jnp.bfloat16
    )
    d_up = (d_hidden * activated).astype(jnp.bfloat16)
    grad_gate = jnp.dot(d_gate, rows_all, preferred_element_type=jnp.float32)
    grad_up = jnp.dot(d_up, rows_all, preferred_element_type=jnp.float32)
    grad_gate, grad_up, grad_down = (
        lax.psum(grad_gate.astype(jnp.bfloat16), "grp").astype(jnp.float32),
        lax.psum(grad_up.astype(jnp.bfloat16), "grp").astype(jnp.float32),
        lax.psum(grad_down.astype(jnp.bfloat16), "grp").astype(jnp.float32),
    )
    return (context[None], talker_out[None], grad_gate, grad_up, grad_down)


def solution(mesh):
    in_specs = (
        P("grp", "ctx", None),
        P("grp", "ctx", None),
        P("grp", "ctx", None),
        P("grp", "ctx"),
        P("grp", None),
        P("grp", None),
        P(),
        P(),
        P("ctx", None),
        P("ctx", None),
        P("ctx", None),
        P("grp", "ctx", None),
    )
    out_specs = (
        P("grp", "ctx", None),
        P("grp", "ctx", None),
        P("ctx", None),
        P("ctx", None),
        P("ctx", None),
    )
    return jax.shard_map(shards, mesh=mesh, in_specs=in_specs, out_specs=out_specs, check_vma=False)
```

profile of v0, /device:TPU:2, one launch (start us, length us, event | category | flops | bytes accessed | tf_op | source)
XLA Modules:
  0.0 526.2 jit_solution(18312703004147743773)
XLA Ops:
  11.6 1.7 convolution_convert_fusion.6
  14.1 37.0 %all-gather = bf16[1,4096]{1,0:T(2,128)(2,1)S(1)} all-gather(bf16[1,128]{1,0:T(2,128)(2,1)S(1)} %get-tuple-element.28), channel_id=2, replica_groups=mesh['ctx'=32,'grp'=8] {'ctx'}, dimensions={1}, use_global_device_ids=true | all-gather | bytes 8448 | tf_op jit(solution)/shard_map/all_gather | solution.py:52
  51.1 2.0 copy.39
  54.6 24.5 %all-gather.12.cloned.1.call-done = bf16[1,4096,256]{1,2,0:T(8,128)(2,1)} async-done(((bf16[1,128,256]{1,2,0:T(8,128)(2,1)}), bf16[1,4096,256]{1,2,0:T(8,128)(2,1)}) %all-gather.12.cloned.1.call-update) | async-done | bytes 2097168 | tf_op jit(solution)/shard_map/all_gather | solution.py:50
  79.1 13.4 %fusion = (f32[128,2,7]{0,2,1:T(8,128)S(1)}, f32[2,4096,128,7]{2,1,3,0:T(8,128)}) fusion(pred[128,4096]{0,1:T(8,128)(4,1)} %fusion.6, bf16[4096,2,128,1]{0,2,3,1:T(8,128)(2,1)} %bitcast.73, bf16[128,2,7,128]{0,3,2,1:T(8,128)(2,1)} %bitcast.72), kind=kOutput, calls=%fused_computation.2 | convolution fusion | flops 1901066496 | bytes 32447488 | tf_op jit(solution)/shard_map/tkgd,skd->tkgs/dot_general | solution.py:61
  92.6 51.8 %all-gather.14.cloned.1.call-done = bf16[1,4096,256]{2,1,0:T(8,128)(2,1)} async-done(((bf16[1,128,256]{2,1,0:T(8,128)(2,1)}), bf16[1,4096,256]{2,1,0:T(8,128)(2,1)}) %all-gather.14.cloned.1.call-update) | async-done | bytes 2097168 | tf_op jit(solution)/shard_map/all_gather | solution.py:51
  144.4 4.1 copy.42
  148.4 13.7 %fusion.1 = f32[128,2,7]{0,2,1:T(8,128)S(1)} fusion(f32[2,4096,128,7]{2,1,3,0:T(8,128)} %get-tuple-element.31, f32[128,2,7]{0,2,1:T(8,128)S(1)} %broadcast_maximum_fusion, pred[128,4096]{0,1:T(8,128)(4,1)} %fusion.6), kind=kLoop, calls=%fused_computation.3 | loop fusion | flops 36698368 | bytes 29898752 | tf_op jit(solution)/shard_map/reduce_sum | solution.py:72
  162.2 14.0 %fusion.16 = bf16[128,2,7,128]{0,3,2,1:T(8,128)(2,1)} fusion(bf16[4096,2,128,1]{0,2,3,1:T(8,128)(2,1)S(1)} %bitcast.74, f32[2,4096,128,7]{2,1,3,0:T(8,128)} %get-tuple-element.31, f32[128,2,7]{0,2,1:T(8,128)S(1)} %broadcast_maximum_fusion, pred[128,4096]{0,1:T(8,128)(4,1)S(1)} %copy-done.1, f32[128,2,7]{0,2,1:T(8,128)S(1)} %fusion.1), kind=kOutput, calls=%fused_computation.28 | convolution fusion | flops 1916207104 | bytes 32454656 | tf_op jit(solution)/shard_map/tkgs,skd->tkgd/dot_general | solution.py:73
  176.2 1.9 multiply_reduce_fusion
  179.1 32.5 %all-gather.10.cloned.1.call-done = bf16[1280,896]{1,0:T(8,128)(2,1)} async-done(((bf16[40,896]{1,0:T(8,128)(2,1)}), bf16[1280,896]{1,0:T(8,128)(2,1)}) %all-gather.10.cloned.1.call-update) | async-done | bytes 2293776 | tf_op jit(solution)/shard_map/all_gather | solution.py:16
  211.7 3.9 convolution_bitcast_fusion
  215.5 63.4 %all-gather.8.cloned.1.call-done = bf16[1280,896]{1,0:T(8,128)(2,1)} async-done(((bf16[40,896]{1,0:T(8,128)(2,1)}), bf16[1280,896]{1,0:T(8,128)(2,1)}) %all-gather.8.cloned.1.call-update) | async-done | bytes 2293776 | tf_op jit(solution)/shard_map/all_gather | solution.py:87
  278.9 2.9 convolution_bitcast_fusion.2
  281.8 1.8 convolution_convert_fusion.2
  284.8 2.1 convolution_convert_fusion.3
  286.9 1.8 convolution_convert_fusion.1
  288.8 4.2 convolution_convert_fusion
  293.0 2.0 copy.45
  295.0 97.3 %all-reduce.4.cloned.1.call-done = (bf16[296,896]{1,0:T(8,128)(2,1)}, bf16[296,896]{1,0:T(8,128)(2,1)}, bf16[296,896]{1,0:T(8,128)(2,1)}) async-done(((bf16[296,896]{1,0:T(8,128)(2,1)}, bf16[296,896]{1,0:T(8,128)(2,1)}, bf16[296,896]{1,0:T(8,128)(2,1)}), (bf16[296,896]{1,0:T(8,128)(2,1)}, bf16[296,896]{1,0:T(8,128)(2,1)}, bf16[296,896]{1,0:T(8,128)(2,1)})) %all-reduce.4.cloned.1.call-update) | async-done | bytes 1591312 | tf_op jit(solution)/shard_map/psum | solution.py:117
  392.2 2.1 convert_element_type.111
  394.4 2.1 convert_element_type.114
  397.5 120.0 %reduce-scatter.5.cloned.1.call-done = bf16[40,896]{1,0:T(8,128)(2,1)} async-done(((bf16[1280,896]{1,0:T(8,128)(2,1)}), bf16[40,896]{1,0:T(8,128)(2,1)}) %reduce-scatter.5.cloned.1.call-update) | async-done | bytes 71696
  517.5 1.8 fusion.11
  (48 shorter events, 9.8 us)
Async XLA Ops:
  7.2 169.0 %copy-start = (bf16[1792,896]{1,0:T(8,128)(2,1)S(1)}, bf16[1792,896]{1,0:T(8,128)(2,1)}, u32[]{:S(2)}) copy-start(bf16[1792,896]{1,0:T(8,128)(2,1)} %param.18) | copy-start | bytes 9633796
  7.2 71.9 %all-gather.12.cloned.1.call-start = ((), (), s32[]{:S(2)}) async-start(), calls=%async_computation.3 | async-start | bytes 2162688 | tf_op jit(solution)/shard_map/all_gather | solution.py:50
  9.0 135.4 %all-gather.14.cloned.1.call-start = ((), (), s32[]{:S(2)}) async-start(), calls=%async_computation.4 | async-start | bytes 2162688 | tf_op jit(solution)/shard_map/all_gather | solution.py:51
  9.7 201.9 %all-gather.10.cloned.1.call-start = ((), (), s32[]{:S(2)}) async-start(), calls=%async_computation.2 | async-start | bytes 2365440 | tf_op jit(solution)/shard_map/all_gather | solution.py:16
  13.4 265.5 %all-gather.8.cloned.1.call-start = ((), (), s32[]{:S(2)}) async-start(), calls=%async_computation.1 | async-start | bytes 2365440 | tf_op jit(solution)/shard_map/all_gather | solution.py:87
  148.4 13.7 %copy-start.1 = (pred[128,4096]{0,1:T(8,128)(4,1)S(1)}, pred[128,4096]{0,1:T(8,128)(4,1)}, u32[]{:S(2)}) copy-start(pred[128,4096]{0,1:T(8,128)(4,1)} %fusion.6) | copy-start | bytes 1572868
  148.4 13.7 %copy-start.2 = (bf16[1,4096,256]{1,2,0:T(8,128)(2,1)S(1)}, bf16[1,4096,256]{1,2,0:T(8,128)(2,1)}, u32[]{:S(2)}) copy-start(bf16[1,4096,256]{1,2,0:T(8,128)(2,1)} %copy.42) | copy-start | bytes 6291460
  176.2 2.0 copy-start.4
  178.9 213.3 %all-reduce.4.cloned.1.call-start = ((), (), s32[]{:S(2)}) async-start(), calls=%async_computation.6 | async-start | bytes 3182592 | tf_op jit(solution)/shard_map/psum | solution.py:117
  278.9 2.9 copy-start.6
  278.9 2.9 copy-start.8
  281.8 1.8 copy-start.7
  284.8 2.1 copy-start.9
  284.8 2.1 copy-start.5
  288.7 228.8 %reduce-scatter.5.cloned.1.call-start = ((), (), s32[]{:S(2)}) async-start(), calls=%async_computation.5 | async-start | bytes 2365440
  392.2 4.2 copy-start.3
Sparse Core Ops, SparseCore 0:
  10.4 68.7 all-gather.11
  81.0 63.3 all-gather.13
  146.8 64.8 all-gather.9
  213.9 64.9 all-gather.7
  288.8 103.3 all-reduce.3
  394.6 122.8 reduce-scatter.4
where the time goes:
time: 527 us; the launch traced here: 526 us
  waiting for transfers between devices  390 us (74%)
  matrix products  50.7 us (10%)
  blocking collectives  37 us (7%)
  other arithmetic  23.5 us (4%)
  between operations  14.2 us (3%)
  local copies, waits for them, and re-layouts  9.99 us (2%)
    unnamed x7, waiting for transfers between devices  121 us
    psum x1, waiting for transfers between devices, shards(): lax.psum(grad_gate.astype(jnp.bfloat16), 'grp').astype(jnp.float32)  97.3 us
    all_gather x1, waiting for transfers between devices, shards(): rows_all = lax.all_gather(normed, 'ctx', axis=0, tiled=True)  63.4 us
    all_gather x1, waiting for transfers between devices, shards(): value_piece = lax.all_gather(values[0], 'ctx', axis=0, tiled=True)  51.8 us
    all_gather x1, blocking collectives, shards(): seg_piece = lax.all_gather(segment_wire, 'ctx', axis=0, tiled=True)  37 us
    all_gather x1, waiting for transfers between devices, collect_cot(): return lax.all_gather(own_cot, 'ctx', axis=0, tiled=True)  32.5 us
    all_gather x1, waiting for transfers between devices, shards(): key_piece = lax.all_gather(keys[0], 'ctx', axis=0, tiled=True)  24.5 us
    dot_general x1, matrix products, shards(): jnp.einsum('tkgs,skd->tkgd', probs.astype(jnp.bfloat16), value_piece.resh...  14 us
  transfers between devices with their start and end apart: 6, of which 6 were waited for; matrix products, arithmetic and copies ran while one was open for 13% of the time, Pallas kernels for 0%

commit v1 on v0

v1 whole, which is shorter than its diff:
```python
import functools
import math

import jax
import jax.numpy as jnp
from jax import lax
from jax.experimental import pallas as pl
from jax.experimental.pallas import tpu as pltpu
from jax.sharding import PartitionSpec as P

HEADS = 14
KV_HEADS = 2
GROUP = HEADS // KV_HEADS
D = 128
TOK = 128
TD = 896
QW = HEADS * D
KW = KV_HEADS * D
SLOTS = 48
NZ = 8
AUX = 16
NEG = -1e30
MESH = pl.DeviceIdType.MESH
BF = jnp.bfloat16
F32 = jnp.float32


class Net:
    def __init__(self, send_sems, recv_sems):
        c = lax.axis_index("ctx")
        self.g = lax.axis_index("grp")
        self.ctx = c
        self.z = c // 4
        self.r = c % 4
        self.y = self.r // 2
        self.k = self.r % 2
        self.send_sems = send_sems
        self.recv_sems = recv_sems
        self.ids = {}
        self.sent = []

    def zmod(self, d):
        return lax.rem(self.z + d + NZ, NZ)

    def dev(self, where):
        z, y, k = self.z, self.y, self.k
        if where == "+":
            z = self.zmod(1)
        elif where == "-":
            z = self.zmod(-1)
        elif where == "y":
            y = 1 - y
        elif where == "c":
            k = 1 - k
        return (z * 4 + y * 2 + k, self.g)

    def copy(self, key, ref, where):
        n = self.ids.setdefault(key, len(self.ids))
        return pltpu.make_async_remote_copy(
            src_ref=ref,
            dst_ref=ref,
            send_sem=self.send_sems.at[n],
            recv_sem=self.recv_sems.at[n],
            device_id=self.dev(where),
            device_id_type=MESH,
        )

    def send(self, key, ref, where):
        copy = self.copy(key, ref, where)
        copy.start()
        self.sent.append(copy)

    def recv(self, key, ref, where):
        self.copy(key, ref, where).wait_recv()

    def drain(self):
        for copy in self.sent:
            copy.wait_send()
        self.sent = []


class Gather:
    def __init__(self, net, name, buf, early):
        self.net, self.name, self.buf, self.early = net, name, buf, early

    def slot(self, d, lane, other_core=False):
        net = self.net
        y = net.y if lane == "o" else 1 - net.y
        k = 1 - net.k if other_core else net.k
        return self.buf.at[net.zmod(d), y * 2 + k]

    def limit(self, way, lane):
        return 4 if (way == "+") == (lane == "o") else 3

    def to_core(self, d, lane):
        self.net.send((self.name, "c", d, lane), self.slot(d, lane), "c")

    def to_z(self, way, lane, step):
        d = -(step - 1) if way == "+" else step - 1
        self.net.send((self.name, way, lane, step), self.slot(d, lane), way)

    def to_y(self, d):
        self.net.send((self.name, "y", d), self.slot(d, "o"), "y")

    def start(self):
        if self.early:
            self.to_y(0)
        self.to_z("+", "o", 1)
        self.to_z("-", "o", 1)
        if not self.early:
            self.to_y(0)
        self.to_core(0, "o")

    def cross(self, d):
        self.net.recv((self.name, "y", d), self.slot(d, "x"), "y")
        if self.early:
            self.to_z("+", "x", 1)
            self.to_z("-", "x", 1)
        self.to_core(d, "x")

    def arrive(self, way, lane, step):
        top = self.limit(way, lane)
        if step > top:
            return
        d = -step if way == "+" else step
        if d == -4:
            d = 4
        self.net.recv((self.name, way, lane, step), self.slot(d, lane), way)
        if step < top:
            self.to_z(way, lane, step + 1)
        if not self.early:
            self.to_y(d)
        self.to_core(d, lane)

    def ring(self, step):
        for lane in ("o", "x") if self.early else ("o",):
            for way in ("+", "-"):
                self.arrive(way, lane, step)

    def crosses(self, step):
        if not self.early:
            for d in around(step):
                self.cross(d)

    def from_core(self, d):
        for lane in ("o", "x"):
            self.net.recv(
                (self.name, "c", d, lane), self.slot(d, lane, other_core=True), "c"
            )


def around(step):
    if step == 0:
        return (0,)
    if step == 4:
        return (4,)
    return (-step, step)


def attend_kernel(
    q_hbm,
    k_hbm,
    v_hbm,
    seg_ref,
    start_ref,
    len_ref,
    w_hbm,
    gain_ref,
    cot_hbm,
    ctx_ref,
    own_ref,
    rows_out,
    cot_out,
    gk,
    gv,
    gr,
    gc,
    q_raw,
    q_buf,
    w_buf,
    cot_buf,
    segq_ref,
    bias_ref,
    m_ref,
    acc_ref,
    send_sems,
    recv_sems,
    local_sems,
):
    net = Net(send_sems, recv_sems)
    z, r = net.z, net.r

    loads = [
        pltpu.make_async_copy(k_hbm.at[0], gk.at[z, r, pl.ds(0, TOK)], local_sems.at[0]),
        pltpu.make_async_copy(v_hbm.at[0], gv.at[z, r], local_sems.at[1]),
        pltpu.make_async_copy(q_hbm.at[0], q_raw, local_sems.at[2]),
        pltpu.make_async_copy(cot_hbm.at[0], cot_buf, local_sems.at[3]),
        pltpu.make_async_copy(w_hbm, w_buf, local_sems.at[4]),
    ]
    for load in loads:
        load.start()

    barrier = pltpu.get_barrier_semaphore()
    for where in ("+", "-", "y", "c"):
        pl.semaphore_signal(
            barrier, inc=1, device_id=net.dev(where), device_id_type=MESH
        )

    seg_row = seg_ref[...].astype(F32)
    gk[z, r, TOK : TOK + AUX, 0:D] = jnp.broadcast_to(seg_row, (AUX, D)).astype(BF)
    gk[z, r, TOK : TOK + AUX, D : 2 * D] = jnp.zeros((AUX, D), BF)

    keys = Gather(net, "k", gk, True)
    vals = Gather(net, "v", gv, False)
    rows = Gather(net, "r", gr, True)
    cots = Gather(net, "g", gc, False)

    loads[0].wait()
    loads[1].wait()
    pl.semaphore_wait(barrier, 4)
    keys.start()
    vals.start()

    segq_ref[...] = jnp.transpose(jnp.broadcast_to(seg_row, (TOK, D)))
    m_ref[...] = jnp.full(m_ref.shape, NEG, F32)
    acc_ref[...] = jnp.zeros(acc_ref.shape, F32)
    loads[2].wait()
    for h in range(HEADS):
        q_buf[h] = q_raw[:, h * D : (h + 1) * D]

    start = start_ref[0, net.ctx] - net.ctx * TOK
    length = len_ref[0, net.ctx]
    slot_id = lax.broadcasted_iota(jnp.int32, (SLOTS, TOK), 0)
    place = lax.broadcasted_iota(jnp.int32, (SLOTS, TOK), 1)
    packer = jnp.where((place - start == slot_id) & (slot_id < length), 1.0, 0.0).astype(BF)
    loads[3].wait()
    gc[z, r] = jnp.dot(packer, cot_buf[...], preferred_element_type=F32).astype(BF)

    factor = math.log2(math.e) / math.sqrt(D)

    def attend(d):
        zc = net.zmod(d)

        def work():
            segq = segq_ref[...]
            for b in range(4):
                seg_k = gk[zc, b, TOK : TOK + AUX, 0:D].astype(F32)[0:1]
                ok = segq == seg_k
                if d == 0:
                    at = (b - r) * TOK
                    kpos = lax.broadcasted_iota(jnp.int32, (TOK, D), 1) + at
                    qpos = lax.broadcasted_iota(jnp.int32, (TOK, D), 0)
                    ok = ok & (kpos <= qpos)
                bias_ref[:, b * TOK : (b + 1) * TOK] = jnp.where(ok, 0.0, NEG)

            def head(i, carry):
                for kv in range(KV_HEADS):
                    h = i + kv * GROUP
                    kc = gk[zc, :, 0:TOK, kv * D : (kv + 1) * D].reshape(4 * TOK, D)
                    vc = gv[zc, :, :, kv * D : (kv + 1) * D].reshape(4 * TOK, D)
                    vc = jnp.concatenate([vc, jnp.ones((4 * TOK, D), BF)], axis=1)
                    s = lax.dot_general(
                        q_buf[h], kc, (((1,), (1,)), ((), ())), preferred_element_type=F32
                    )
                    s = s * factor + bias_ref[...]
                    m_old = m_ref[h]
                    m_new = jnp.maximum(m_old, jnp.max(s, axis=1, keepdims=True))
                    p = jnp.exp2(s - jnp.concatenate([m_new] * 4, axis=1)).astype(BF)
                    alpha = jnp.exp2(m_old - m_new)
                    m_ref[h] = m_new
                    acc_ref[h] = acc_ref[h] * jnp.concatenate([alpha, alpha], axis=1) + jnp.dot(
                        p, vc, preferred_element_type=F32
                    )
                return carry

            lax.fori_loop(0, GROUP, head, 0)

        if d == 0:
            work()
        else:
            pl.when(zc < z)(work)

    def attend_step(step):
        for d in around(step):
            keys.from_core(d)
            vals.from_core(d)
            attend(d)

    keys.cross(0)
    vals.crosses(0)
    for step in range(1, 5):
        keys.ring(step)
        vals.ring(step)
        if step == 4:
            cots.start()
        attend_step(step - 1)
        vals.crosses(step)
    cots.ring(1)
    cots.crosses(0)
    attend_step(4)

    loads[4].wait()
    for h in range(HEADS):
        acc = acc_ref[h]
        ctx_ref[0, :, h * D : (h + 1) * D] = (acc[:, 0:D] / acc[:, D : 2 * D]).astype(BF)
    packed = jnp.dot(packer, ctx_ref[0], preferred_element_type=F32).astype(BF)
    own = jnp.dot(packed, w_buf[...], preferred_element_type=F32).astype(BF)
    own_ref[...] = own
    own = own.astype(F32)
    scale = lax.rsqrt(jnp.mean(own * own, axis=-1, keepdims=True) + 1e-06)
    gr[z, r] = (own * scale * gain_ref[...]).astype(BF)

    rows.start()
    rows.cross(0)
    cots.ring(2)
    cots.crosses(1)
    for step in range(1, 5):
        rows.ring(step)
        if step < 3:
            cots.ring(step + 2)
            cots.crosses(step + 1)
    cots.crosses(4)
    for step in range(5):
        for d in around(step):
            rows.from_core(d)
            cots.from_core(d)
    outs = [
        pltpu.make_async_copy(gr, rows_out, local_sems.at[5]),
        pltpu.make_async_copy(gc, cot_out, local_sems.at[6]),
    ]
    for out in outs:
        out.start()
    net.drain()
    for out in outs:
        out.wait()


def attend_call(queries, keys, values, segment_ids, turn_start, turn_len, w_proj, gain, cotangent):
    hbm = pl.BlockSpec(memory_space=pl.ANY)
    vmem = pl.BlockSpec(memory_space=pltpu.VMEM)
    smem = pl.BlockSpec(memory_space=pltpu.SMEM)
    wide = (NZ, 4, SLOTS, TD)
    return pl.pallas_call(
        attend_kernel,
        name="attend",
        out_shape=[
            jax.ShapeDtypeStruct((1, TOK, QW), BF),
            jax.ShapeDtypeStruct((SLOTS, TD), BF),
            jax.ShapeDtypeStruct(wide, BF),
            jax.ShapeDtypeStruct(wide, BF),
        ],
        in_specs=[hbm, hbm, hbm, vmem, smem, smem, hbm, vmem, hbm],
        out_specs=[vmem, vmem, hbm, hbm],
        scratch_shapes=[
            pltpu.VMEM((NZ, 4, TOK + AUX, KW), BF),
            pltpu.VMEM((NZ, 4, TOK, KW), BF),
            pltpu.VMEM(wide, BF),
            pltpu.VMEM(wide, BF),
            pltpu.VMEM((TOK, QW), BF),
            pltpu.VMEM((HEADS, TOK, D), BF),
            pltpu.VMEM((QW, TD), BF),
            pltpu.VMEM((TOK, TD), BF),
            pltpu.VMEM((TOK, D), F32),
            pltpu.VMEM((TOK, 4 * TOK), F32),
            pltpu.VMEM((HEADS, TOK, D), F32),
            pltpu.VMEM((HEADS, TOK, 2 * D), F32),
            pltpu.SemaphoreType.DMA((128,)),
            pltpu.SemaphoreType.DMA((128,)),
            pltpu.SemaphoreType.DMA((8,)),
        ],
        compiler_params=pltpu.CompilerParams(
            collective_id=1, has_side_effects=True, vmem_limit_bytes=48 << 20
        ),
    )(queries, keys, values, segment_ids, turn_start, turn_len, w_proj, gain, cotangent)


def shards(
    queries,
    keys,
    values,
    segment_ids,
    turn_start,
    turn_len,
    w_proj,
    gain,
    gate_w,
    up_w,
    down_w,
    cotangent,
):
    context, own_rows, rows_all, cot_all = attend_call(
        queries, keys, values, segment_ids, turn_start, turn_len, w_proj, gain[None], cotangent
    )
    rows_all = rows_all.reshape(NZ * 4 * SLOTS, TD)
    cot_all = cot_all.reshape(NZ * 4 * SLOTS, TD)
    own_rows = own_rows.astype(F32)
    ctx_index = lax.axis_index("ctx")
    start = turn_start[0, ctx_index] - ctx_index * TOK
    slot_id = jnp.arange(SLOTS, dtype=jnp.int32)[:, None]
    place = jnp.arange(TOK, dtype=jnp.int32)[None, :]
    packer = ((place - start == slot_id) & (slot_id < turn_len[0, ctx_index])).astype(BF)
    contract_last = (((1,), (1,)), ((), ()))
    contract_first = (((0,), (0,)), ((), ()))
    gate_pre = lax.dot_general(gate_w, rows_all, contract_last, preferred_element_type=jnp.float32)
    up_pre = lax.dot_general(up_w, rows_all, contract_last, preferred_element_type=jnp.float32)
    sigmoid_gate = jax.nn.sigmoid(gate_pre)
    activated = gate_pre * sigmoid_gate
    hidden_t = (activated * up_pre).astype(jnp.bfloat16)
    ffn_rows = lax.psum_scatter(
        lax.dot_general(
            hidden_t, down_w, contract_first, preferred_element_type=jnp.float32
        ).astype(jnp.bfloat16),
        "ctx",
        scatter_dimension=0,
        tiled=True,
    ).astype(jnp.float32)
    out_rows = (own_rows + ffn_rows).astype(jnp.bfloat16)
    talker_out = lax.dot_general(
        packer, out_rows, contract_first, preferred_element_type=jnp.float32
    ).astype(jnp.bfloat16)
    d_hidden = lax.dot_general(down_w, cot_all, contract_last, preferred_element_type=jnp.float32)
    grad_down = jnp.dot(hidden_t, cot_all, preferred_element_type=jnp.float32)
    d_gate = (d_hidden * up_pre * sigmoid_gate * (1.0 + gate_pre * (1.0 - sigmoid_gate))).astype(
        jnp.bfloat16
    )
    d_up = (d_hidden * activated).astype(jnp.bfloat16)
    grad_gate = jnp.dot(d_gate, rows_all, preferred_element_type=jnp.float32)
    grad_up = jnp.dot(d_up, rows_all, preferred_element_type=jnp.float32)
    grad_gate, grad_up, grad_down = (
        lax.psum(grad_gate.astype(jnp.bfloat16), "grp").astype(jnp.float32),
        lax.psum(grad_up.astype(jnp.bfloat16), "grp").astype(jnp.float32),
        lax.psum(grad_down.astype(jnp.bfloat16), "grp").astype(jnp.float32),
    )
    return (context, talker_out[None], grad_gate, grad_up, grad_down)


def solution(mesh):
    in_specs = (
        P("grp", "ctx", None),
        P("grp", "ctx", None),
        P("grp", "ctx", None),
        P("grp", "ctx"),
        P("grp", None),
        P("grp", None),
        P(),
        P(),
        P("ctx", None),
        P("ctx", None),
        P("ctx", None),
        P("grp", "ctx", None),
    )
    out_specs = (
        P("grp", "ctx", None),
        P("grp", "ctx", None),
        P("ctx", None),
        P("ctx", None),
        P("ctx", None),
    )
    return jax.shard_map(shards, mesh=mesh, in_specs=in_specs, out_specs=out_specs, check_vma=False)
```

time: 527 us -> 252 us (0.48)
  waiting for transfers between devices: 390 us -> 131 us
  Pallas kernels: 0 us -> 76 us
  blocking collectives: 37 us -> 0 us
  matrix products: 50.7 us -> 15.1 us
  other arithmetic: 23.5 us -> 4.92 us
    all_gather x4 -> x0, waiting for transfers between devices: 172 us -> none  [the longest x1 63.4 us: shards(): rows_all = lax.all_gather(normed, 'ctx', axis=0, tiled=True)]
    unnamed x7 -> x2, waiting for transfers between devices: 121 us -> 0.03 us
    pallas_call x0 -> x1, Pallas kernels: none -> 76 us  [attend_call(): pl.pallas_call(attend_kernel, name='attend', out_shape=[jax.ShapeDtypeStr...]
    all_gather x1 -> x0, blocking collectives: 37 us -> none  [shards(): seg_piece = lax.all_gather(segment_wire, 'ctx', axis=0, tiled=True)]
    dot_general x4 -> x0, matrix products: 31.1 us -> none  [the longest x1 14 us: shards(): jnp.einsum('tkgs,skd->tkgd', probs.astype(jnp.bfloat16), value_piece.resh...]
    reduce_scatter x0 -> x1, waiting for transfers between devices: none -> 23.1 us  [shards(): lax.psum_scatter(lax.dot_general(hidden_t, down_w, contract_first, prefer...]
    reduce_sum x1 -> x0, other arithmetic: 13.7 us -> none  [shards(): new_sum = jnp.sum(probs, axis=-1)]
    psum x1, waiting for transfers between devices: 97.3 us -> 108 us  [shards(): lax.psum(grad_gate.astype(jnp.bfloat16), 'grp').astype(jnp.float32)]
  transfers between devices with their start and end apart: 6 -> 2, of which waited for: 6 -> 2; matrix products, arithmetic and copies ran while one was open for 13% -> 4% of each run, Pallas kernels for 0% -> 0%
where the time goes in v1:
time: 252 us
  waiting for transfers between devices  131 us (52%)
  Pallas kernels  76 us (30%)
  between operations  16.2 us (6%)
  matrix products  15.1 us (6%)
  local copies, waits for them, and re-layouts  8.85 us (4%)
  other arithmetic  4.92 us (2%)
    psum x1, waiting for transfers between devices, shards(): lax.psum(grad_gate.astype(jnp.bfloat16), 'grp').astype(jnp.float32)  108 us
    pallas_call x1, Pallas kernels, attend_call(): pl.pallas_call(attend_kernel, name='attend', out_shape=[jax.ShapeDtypeStr...  76 us
    reduce_scatter x1, waiting for transfers between devices, shards(): lax.psum_scatter(lax.dot_general(hidden_t, down_w, contract_first, prefer...  23.1 us
    unnamed x31, local copies, waits for them, and re-layouts  7.53 us
  transfers between devices with their start and end apart: 2, of which 2 were waited for; matrix products, arithmetic and copies ran while one was open for 4% of the time, Pallas kernels for 0%

profile of v1, /device:TPU:2, one launch (start us, length us, event | category | flops | bytes accessed | tf_op | source)
XLA Modules:
  0.0 251.9 jit_solution(18392147664783724382)
XLA Ops:
  8.1 0.7 broadcast_in_dim.8.gain_ref
  8.8 1.0 copy-done.1
  9.8 0.9 copy-done.2
  10.8 0.8 copy-done.3
  11.6 0.8 copy-done.4
  12.4 0.7 copy-done.5
  13.1 0.7 copy-done.7
  13.8 0.7 copy-done.9
  14.4 76.0 %attend.1 = (bf16[1,128,1792]{2,1,0:T(8,128)(2,1)S(1)}, bf16[48,896]{1,0:T(8,128)(2,1)S(1)}, bf16[8,4,48,896]{3,2,1,0:T(8,128)(2,1)S(1)}, bf16[8,4,48,896]{3,2,1,0:T(8,128)(2,1)}) custom-call(bf16[1,128,1792]{2,1,0:T(8,128)(2,1)S(1)} %copy-done.1, bf16[1,128,256]{2,1,0:T(8,128)(2,1)S(1)} %copy-done.3, bf16[1,128,256]{2,1,0:T(8,128)(2,1)S(1)} %copy-done.4, ...), custom_call_target="tpu_custom_call" | custom-call | tf_op jit(solution)/shard_map/attend/pallas_call | solution.py:343
  90.5 1.1 convolution_bitcast_fusion.2
  91.6 1.3 multiply_convert_fusion.2
  93.4 1.1 convolution_bitcast_fusion
  94.6 2.0 convolution_convert_fusion.2
  96.6 2.4 convolution_convert_fusion.3
  98.9 1.9 convolution_convert_fusion.1
  100.9 3.3 %convolution_convert_fusion = bf16[1536,896]{1,0:T(8,128)(2,1)} fusion(bf16[296,1536]{1,0:T(8,128)(2,1)S(1)} %get-tuple-element.16, bf16[296,896]{1,0:T(8,128)(2,1)S(1)} %copy-done), kind=kOutput, calls=%fused_computation | convolution fusion | flops 816119808 | bytes 4192256 | tf_op jit(solution)/shard_map/dot_general | solution.py:410
  106.2 0.7 iota_compare_fusion.1
  106.8 107.6 %all-reduce.3.cloned.1.call-done = (bf16[296,896]{1,0:T(8,128)(2,1)}, bf16[296,896]{1,0:T(8,128)(2,1)}, bf16[296,896]{1,0:T(8,128)(2,1)}) async-done(((bf16[296,896]{1,0:T(8,128)(2,1)}, bf16[296,896]{1,0:T(8,128)(2,1)}, bf16[296,896]{1,0:T(8,128)(2,1)}), (bf16[296,896]{1,0:T(8,128)(2,1)}, bf16[296,896]{1,0:T(8,128)(2,1)}, bf16[296,896]{1,0:T(8,128)(2,1)})) %all-reduce.3.cloned.1.call-update) | async-done | bytes 1591312 | tf_op jit(solution)/shard_map/psum | solution.py:430
  214.4 2.2 convert_element_type.51
  216.6 1.0 convert_element_type.54
  217.6 1.0 convert_element_type.56
  218.7 23.1 %reduce-scatter.2.cloned.1.call-done = bf16[48,896]{1,0:T(8,128)(2,1)} async-done(((bf16[1536,896]{1,0:T(8,128)(2,1)}), bf16[48,896]{1,0:T(8,128)(2,1)}) %reduce-scatter.2.cloned.1.call-update) | async-done | bytes 86032 | tf_op jit(solution)/shard_map/reduce_scatter | solution.py:409
  241.8 1.9 fusion.1
  243.7 0.8 copy.21
  (29 shorter events, 1.9 us)
Async XLA Ops:
  8.0 84.9 %copy-start = (bf16[296,896]{1,0:T(8,128)(2,1)S(1)}, bf16[296,896]{1,0:T(8,128)(2,1)}, u32[]{:S(2)}) copy-start(bf16[296,896]{1,0:T(8,128)(2,1)} %param.22) | copy-start | bytes 1591300
  8.0 206.4 %all-reduce.3.cloned.1.call-start = ((), (), s32[]{:S(2)}) async-start(), calls=%async_computation.2 | async-start | bytes 3182592 | tf_op jit(solution)/shard_map/psum | solution.py:430
  8.8 1.0 copy-start.1
  9.8 0.9 copy-start.2
  10.8 0.8 copy-start.3
  11.6 0.8 copy-start.4
  12.4 0.7 copy-start.5
  13.1 0.7 copy-start.7
  13.7 0.7 copy-start.9
  14.4 76.1 %copy-start.13 = (bf16[296,896]{1,0:T(8,128)(2,1)S(1)}, bf16[296,896]{1,0:T(8,128)(2,1)}, u32[]{:S(2)}) copy-start(bf16[296,896]{1,0:T(8,128)(2,1)} %param.20) | copy-start | bytes 1591300
  90.5 1.2 copy-start.14
  91.6 1.8 copy-start.12
  100.9 140.9 %reduce-scatter.2.cloned.1.call-start = ((), (), s32[]{:S(2)}) async-start(), calls=%async_computation.1 | async-start | bytes 2838528 | tf_op jit(solution)/shard_map/reduce_scatter | solution.py:409
  104.2 0.7 copy-start.6
  104.2 0.7 copy-start.8
  214.4 2.2 copy-start.11
  214.4 3.2 %copy-start.10 = (bf16[296,896]{1,0:T(8,128)(2,1)S(1)}, bf16[296,896]{1,0:T(8,128)(2,1)}, u32[]{:S(2)}) copy-start(bf16[296,896]{1,0:T(8,128)(2,1)} %get-tuple-element.15) | copy-start | bytes 1591300
Sparse Core Ops, SparseCore 0:
  101.0 113.3 all-reduce.2
Sparse Core Ops, SparseCore 1:
  104.4 137.4 reduce-scatter.1

commit v2 on v1

--- a/solution.py
+++ b/solution.py
@@ -18,6 +18,14 @@
 KW = KV_HEADS * D
 SLOTS = 48
 NZ = 8
+NX = 4
+FFD = 296
+GROWS = 896
+A_ROWS = 512
+A_PART = 64
+B_PART = 48
+B_HALF = (32, 16)
+CHUNK = 256
 AUX = 16
 NEG = -1e30
 MESH = pl.DeviceIdType.MESH
@@ -28,12 +36,14 @@
 class Net:
     def __init__(self, send_sems, recv_sems):
         c = lax.axis_index("ctx")
-        self.g = lax.axis_index("grp")
+        g = lax.axis_index("grp")
         self.ctx = c
         self.z = c // 4
         self.r = c % 4
         self.y = self.r // 2
         self.k = self.r % 2
+        self.x = g // 2
+        self.h = g % 2
         self.send_sems = send_sems
         self.recv_sems = recv_sems
         self.ids = {}
@@ -42,8 +52,11 @@
     def zmod(self, d):
         return lax.rem(self.z + d + NZ, NZ)
 
+    def xmod(self, d):
+        return lax.rem(self.x + d + NX, NX)
+
     def dev(self, where):
-        z, y, k = self.z, self.y, self.k
+        z, y, k, x, h = self.z, self.y, self.k, self.x, self.h
         if where == "+":
             z = self.zmod(1)
         elif where == "-":
@@ -52,26 +65,38 @@
             y = 1 - y
         elif where == "c":
             k = 1 - k
-        return (z * 4 + y * 2 + k, self.g)
-
-    def copy(self, key, ref, where):
+        elif where == "x+":
+            x = self.xmod(1)
+        elif where == "x-":
+            x = self.xmod(-1)
+        elif where == "h":
+            h = 1 - h
+        return (z * 4 + y * 2 + k, x * 2 + h)
+
+    def greet(self, barrier, places):
+        for where in places:
+            pl.semaphore_signal(
+                barrier, inc=1, device_id=self.dev(where), device_id_type=MESH
+            )
+
+    def copy(self, key, src, dst, where):
         n = self.ids.setdefault(key, len(self.ids))
         return pltpu.make_async_remote_copy(
-            src_ref=ref,
-            dst_ref=ref,
+            src_ref=src,
+            dst_ref=dst,
             send_sem=self.send_sems.at[n],
             recv_sem=self.recv_sems.at[n],
             device_id=self.dev(where),
             device_id_type=MESH,
         )
 
-    def send(self, key, ref, where):
-        copy = self.copy(key, ref, where)
+    def send(self, key, src, where, dst=None):
+        copy = self.copy(key, src, src if dst is None else dst, where)
         copy.start()
         self.sent.append(copy)
 
     def recv(self, key, ref, where):
-        self.copy(key, ref, where).wait_recv()
+        self.copy(key, ref, ref, where).wait_recv()
 
     def drain(self):
         for copy in self.sent:
@@ -201,10 +226,7 @@
         load.start()
 
     barrier = pltpu.get_barrier_semaphore()
-    for where in ("+", "-", "y", "c"):
-        pl.semaphore_signal(
-            barrier, inc=1, device_id=net.dev(where), device_id_type=MESH
-        )
+    net.greet(barrier, ("+", "-", "y", "c"))
 
     seg_row = seg_ref[...].astype(F32)
     gk[z, r, TOK : TOK + AUX, 0:D] = jnp.broadcast_to(seg_row, (AUX, D)).astype(BF)
@@ -374,6 +396,410 @@
     )(queries, keys, values, segment_ids, turn_start, turn_len, w_proj, gain, cotangent)
 
 
+class GradSum:
+    def __init__(self, net, g32, res, sa, ra, sa3, sah, rah, sb, rb, b32, sbx, rbx, sb3):
+        self.net, self.g32, self.res = net, g32, res
+        self.sa, self.ra, self.sa3, self.sah, self.rah = sa, ra, sa3, sah, rah
+        self.sb, self.rb, self.b32, self.sbx, self.rbx, self.sb3 = sb, rb, b32, sbx, rbx, sb3
+
+    def a_rows(self, x, h, count=1):
+        return pl.ds(pl.multiple_of((x * 2 + h) * A_PART, A_PART), count * A_PART)
+
+    def b_rows(self, h, x, half=None):
+        at = A_ROWS + (h * NX + x) * B_PART
+        size = B_PART
+        if half is not None:
+            at, size = at + half * B_HALF[0], B_HALF[half]
+        return pl.ds(pl.multiple_of(at, 16), size)
+
+    def start(self):
+        net = self.net
+        self.sb[...] = self.g32[
+            pl.ds(pl.multiple_of(A_ROWS + (1 - net.h) * NX * B_PART, 16), NX * B_PART)
+        ].astype(BF)
+        net.send("b0", self.sb, "h", self.rb)
+        for i in range(NX):
+            for h in range(2):
+                at = (i * 2 + h) * A_PART
+                self.sa[i, h] = self.g32[at : at + A_PART].astype(BF)
+        far = net.xmod(2)
+        net.send("a1+", self.sa.at[far, 0], "x+", self.ra.at[0])
+        net.send("a1-", self.sa.at[far, 1], "x-", self.ra.at[1])
+        net.send("a2+", self.sa.at[net.xmod(1), 1], "x+", self.ra.at[2])
+        net.send("a2-", self.sa.at[net.xmod(-1), 0], "x-", self.ra.at[3])
+
+    def a_pass(self):
+        net = self.net
+        for n, (way, d, half) in enumerate((("+", 1, 0), ("-", -1, 1))):
+            net.recv("a1" + way, self.ra.at[n], "x" + way)
+            own = self.g32[self.a_rows(net.xmod(d), half)]
+            self.sa3[n] = (own + self.ra[n].astype(F32)).astype(BF)
+            net.send("a3" + way, self.sa3.at[n], "x" + way, self.ra.at[4 + n])
+
+    def a_cross(self):
+        net = self.net
+        net.recv("a2+", self.ra.at[2], "x+")
+        net.recv("a2-", self.ra.at[3], "x-")
+        net.recv("a3+", self.ra.at[4], "x+")
+        net.recv("a3-", self.ra.at[5], "x-")
+        for half, (one, two) in enumerate(((3, 4), (2, 5))):
+            rows = self.a_rows(net.x, half)
+            self.g32[rows] = self.g32[rows] + self.ra[one].astype(F32) + self.ra[two].astype(F32)
+        self.sah[...] = self.g32[self.a_rows(net.x, 1 - net.h)].astype(BF)
+        net.send("ah", self.sah, "h", self.rah)
+
+    def a_final(self):
+        net = self.net
+        net.recv("ah", self.rah, "h")
+        rows = self.a_rows(net.x, net.h)
+        self.res[rows] = (self.g32[rows] + self.rah[...].astype(F32)).astype(BF)
+        for key, where in (("e0", "h"), ("e1+", "x+"), ("e1-", "x-")):
+            net.send(key, self.res.at[rows], where)
+
+    def a_spread(self):
+        net = self.net
+        rows = self.res.at[self.a_rows(net.x, 1 - net.h)]
+        net.recv("e0", rows, "h")
+        net.send("e2+", rows, "x+")
+        net.send("e2-", rows, "x-")
+
+    def a_forward(self):
+        net = self.net
+        for way, d, half in (("+", -1, 0), ("-", 1, 1)):
+            x = net.xmod(d)
+            net.recv("e1" + way, self.res.at[self.a_rows(x, net.h)], "x" + way)
+            net.recv("e2" + way, self.res.at[self.a_rows(x, 1 - net.h)], "x" + way)
+            net.send("f" + way, self.res.at[self.a_rows(x, half)], "x" + way)
+
+    def a_end(self):
+        net = self.net
+        for way, half in (("+", 0), ("-", 1)):
+            net.recv("f" + way, self.res.at[self.a_rows(net.xmod(2), half)], "x" + way)
+
+    def b_half(self, half):
+        return pl.ds(0 if half == 0 else B_HALF[0], B_HALF[half])
+
+    def b_start(self):
+        net = self.net
+        net.recv("b0", self.rb, "h")
+        for i in range(NX):
+            at = slice(i * B_PART, (i + 1) * B_PART)
+            own = self.g32[self.b_rows(net.h, i)]
+            total = own + self.rb[at].astype(F32)
+            self.b32[i] = total
+            self.sbx[i] = total.astype(BF)
+        for n, (key, way, d, half) in enumerate(
+            (("b1+", "+", 2, 0), ("b1-", "-", 2, 1), ("b2+", "+", 1, 1), ("b2-", "-", -1, 0))
+        ):
+            net.send(
+                key,
+                self.sbx.at[net.xmod(d), self.b_half(half)],
+                "x" + way,
+                self.rbx.at[n, pl.ds(0, B_HALF[half])],
+            )
+
+    def b_pass(self):
+        net = self.net
+        for n, (way, d, half) in enumerate((("+", 1, 0), ("-", -1, 1))):
+            size = B_HALF[half]
+            net.recv("b1" + way, self.rbx.at[n, pl.ds(0, size)], "x" + way)
+            own = self.b32[net.xmod(d), self.b_half(half)]
+            self.sb3[n, 0:size] = (own + self.rbx[n, 0:size].astype(F32)).astype(BF)
+            net.send(
+                "b3" + way,
+                self.sb3.at[n, pl.ds(0, size)],
+                "x" + way,
+                self.rbx.at[4 + n, pl.ds(0, size)],
+            )
+
+    def b_final(self):
+        net = self.net
+        net.recv("b2+", self.rbx.at[2, pl.ds(0, B_HALF[1])], "x+")
+        net.recv("b2-", self.rbx.at[3, pl.ds(0, B_HALF[0])], "x-")
+        net.recv("b3+", self.rbx.at[4, pl.ds(0, B_HALF[0])], "x+")
+        net.recv("b3-", self.rbx.at[5, pl.ds(0, B_HALF[1])], "x-")
+        for half, (one, two) in enumerate(((3, 4), (2, 5))):
+            size = B_HALF[half]
+            total = (
+                self.b32[net.x, self.b_half(half)]
+                + self.rbx[one, 0:size].astype(F32)
+                + self.rbx[two, 0:size].astype(F32)
+            )
+            self.res[self.b_rows(net.h, net.x, half)] = total.astype(BF)
+        rows = self.res.at[self.b_rows(net.h, net.x)]
+        for key, where in (("q+", "x+"), ("q-", "x-"), ("p0", "h")):
+            net.send(key, rows, where)
+
+    def b_forward(self):
+        net = self.net
+        for n, (way, d, half) in enumerate((("+", -1, 0), ("-", 1, 1))):
+            x = net.xmod(d)
+            rows = self.res.at[self.b_rows(net.h, x)]
+            net.recv("q" + way, rows, "x" + way)
+            net.send("s" + way, self.res.at[self.b_rows(net.h, x, half)], "x" + way)
+            net.send("p%d" % (n + 1), rows, "h")
+
+    def b_cross(self):
+        net = self.net
+        x = net.xmod(2)
+        for way, half in (("+", 0), ("-", 1)):
+            net.recv("s" + way, self.res.at[self.b_rows(net.h, x, half)], "x" + way)
+        net.send("p3", self.res.at[self.b_rows(net.h, x)], "h")
+
+    def b_end(self):
+        net = self.net
+        for n, d in enumerate((0, -1, 1, 2)):
+            net.recv("p%d" % n, self.res.at[self.b_rows(1 - net.h, net.xmod(d))], "h")
+
+
+class RowSum:
+    def __init__(self, net, part, from_core, stage, land, ys, yr):
+        self.net, self.part, self.from_core = net, part, from_core
+        self.stage, self.land, self.ys, self.yr = stage, land, ys, yr
+        self.at = {}
+        for way in ("+", "-"):
+            for lane in ("o", "x"):
+                for step in range(1, self.limit(way, lane) + 1):
+                    self.at[way, lane, step] = len(self.at)
+
+    def limit(self, way, lane):
+        return 4 if (way == "+") == (lane == "o") else 3
+
+    def swap(self, d):
+        net = self.net
+        z = net.zmod(d)
+        net.send(("c", d), self.part.at[1 - net.k, z], "c", self.from_core.at[z])
+
+    def swapped(self, d):
+        self.net.recv(("c", d), self.from_core.at[self.net.zmod(d)], "c")
+
+    def own(self, d, lane):
+        net = self.net
+        z = net.zmod(d)
+        y = net.y if lane == "o" else 1 - net.y
+        return self.part[net.k, z, y].astype(F32) + self.from_core[z, y].astype(F32)
+
+    def landed(self, way, lane, step):
+        n = self.at[way, lane, step]
+        self.net.recv(("z", way, lane, step), self.land.at[n], way)
+        return self.land[n].astype(F32)
+
+    def step(self, step):
+        for lane in ("o", "x"):
+            for way in ("+", "-"):
+                top = self.limit(way, lane)
+                if step > top:
+                    continue
+                left = top - step + 1
+                d = left if way == "+" or left == 4 else -left
+                total = self.own(d, lane)
+                if step > 1:
+                    total = total + self.landed(way, lane, step - 1)
+                n = self.at[way, lane, step]
+                self.stage[n] = total.astype(BF)
+                self.net.send(("z", way, lane, step), self.stage.at[n], way, self.land.at[n])
+
+    def across(self):
+        total = self.own(0, "x")
+        for way in ("+", "-"):
+            total = total + self.landed(way, "x", self.limit(way, "x"))
+        self.ys[...] = total.astype(BF)
+        self.net.send("y", self.ys, "y", self.yr)
+
+    def result(self):
+        total = self.own(0, "o")
+        for way in ("+", "-"):
+            total = total + self.landed(way, "o", self.limit(way, "o"))
+        self.net.recv("y", self.yr, "y")
+        return total + self.yr[...].astype(F32)
+
+
+def talk_kernel(
+    rows_hbm,
+    cot_hbm,
+    own_ref,
+    start_ref,
+    len_ref,
+    gate_ref,
+    up_ref,
+    down_ref,
+    out_ref,
+    grads_out,
+    rows,
+    cots,
+    hid,
+    d_gate,
+    d_up,
+    hid_rows,
+    g32,
+    res,
+    sa,
+    ra,
+    sa3,
+    sah,
+    rah,
+    sb,
+    rb,
+    b32,
+    sbx,
+    rbx,
+    sb3,
+    part,
+    from_core,
+    stage,
+    land,
+    ys,
+    yr,
+    send_sems,
+    recv_sems,
+    local_sems,
+):
+    net = Net(send_sems, recv_sems)
+    loads = [
+        pltpu.make_async_copy(rows_hbm, rows, local_sems.at[0]),
+        pltpu.make_async_copy(cot_hbm, cots, local_sems.at[1]),
+    ]
+    for load in loads:
+        load.start()
+    barrier = pltpu.get_barrier_semaphore()
+    places = ("+", "-", "y", "c", "x+", "x-", "h")
+    net.greet(barrier, places)
+    for load in loads:
+        load.wait()
+
+    nt = (((1,), (1,)), ((), ()))
+
+    def chunk(i, carry):
+        at = pl.ds(pl.multiple_of(i * CHUNK, CHUNK), CHUNK)
+        row = rows[at]
+        cot = cots[at]
+        gate = lax.dot_general(gate_ref[...], row, nt, preferred_element_type=F32)
+        up = lax.dot_general(up_ref[...], row, nt, preferred_element_type=F32)
+        d_hidden = lax.dot_general(down_ref[...], cot, nt, preferred_element_type=F32)
+        sig = jax.nn.sigmoid(gate)
+        act = gate * sig
+        hidden = act * up
+        hid[:, at] = hidden.astype(BF)
+        hid_rows[at] = jnp.transpose(hidden).astype(BF)
+        d_gate[:, at] = (d_hidden * up * sig * (1.0 + gate * (1.0 - sig))).astype(BF)
+        d_up[:, at] = (d_hidden * act).astype(BF)
+        return carry
+
+    lax.fori_loop(0, rows.shape[0] // CHUNK, chunk, 0)
+
+    for n, (left, right) in enumerate(((hid, cots), (d_gate, rows), (d_up, rows))):
+        g32[n * FFD : (n + 1) * FFD] = jnp.dot(
+            left[...], right[...], preferred_element_type=F32
+        )
+    g32[3 * FFD :] = jnp.zeros((GROWS - 3 * FFD, TD), F32)
+
+    grads = GradSum(net, g32, res, sa, ra, sa3, sah, rah, sb, rb, b32, sbx, rbx, sb3)
+    sums = RowSum(net, part, from_core, stage, land, ys, yr)
+    pl.semaphore_wait(barrier, len(places))
+    grads.start()
+
+    def ffn(d):
+        z = net.zmod(d)
+        at = pl.ds(pl.multiple_of(z * 4 * SLOTS, 4 * SLOTS), 4 * SLOTS)
+        total = jnp.dot(hid_rows[at], down_ref[...], preferred_element_type=F32).astype(BF)
+        for b in range(4):
+            part[b % 2, z, b // 2] = total[b * SLOTS : (b + 1) * SLOTS]
+        sums.swap(d)
+
+    for d in (4, 3, -3):
+        ffn(d)
+    grads.a_pass()
+    for d in (2, -2):
+        ffn(d)
+    for d in (4, 3, -3):
+        sums.swapped(d)
+    sums.step(1)
+    for d in (1, -1, 0):
+        ffn(d)
+    grads.b_start()
+    for d in (2, -2):
+        sums.swapped(d)
+    sums.step(2)
+    grads.a_cross()
+    for d in (1, -1, 0):
+        sums.swapped(d)
+    sums.step(3)
+    grads.b_pass()
+    grads.a_final()
+    sums.step(4)
+    grads.b_final()
+    grads.a_spread()
+    sums.across()
+    grads.b_forward()
+    grads.a_forward()
+    grads.b_cross()
+
+    start = start_ref[0, net.ctx] - net.ctx * TOK
+    length = len_ref[0, net.ctx]
+    place = lax.broadcasted_iota(jnp.int32, (TOK, SLOTS), 0)
+    slot_id = lax.broadcasted_iota(jnp.int32, (TOK, SLOTS), 1)
+    spread = jnp.where((place - start == slot_id) & (slot_id < length), 1.0, 0.0).astype(BF)
+    out_rows = (own_ref[...].astype(F32) + sums.result()).astype(BF)
+    out_ref[0] = jnp.dot(spread, out_rows, preferred_element_type=F32).astype(BF)
+
+    grads.a_end()
+    grads.b_end()
+    save = pltpu.make_async_copy(res, grads_out, local_sems.at[2])
+    save.start()
+    net.drain()
+    save.wait()
+
+
+def talk_call(rows, cots, own, turn_start, turn_len, gate_w, up_w, down_w):
+    hbm = pl.BlockSpec(memory_space=pl.ANY)
+    vmem = pl.BlockSpec(memory_space=pltpu.VMEM)
+    smem = pl.BlockSpec(memory_space=pltpu.SMEM)
+    total = NZ * 4 * SLOTS
+    return pl.pallas_call(
+        talk_kernel,
+        name="talk",
+        out_shape=[
+            jax.ShapeDtypeStruct((1, TOK, TD), BF),
+            jax.ShapeDtypeStruct((GROWS, TD), BF),
+        ],
+        in_specs=[hbm, hbm, vmem, smem, smem, vmem, vmem, vmem],
+        out_specs=[vmem, hbm],
+        scratch_shapes=[
+            pltpu.VMEM((total, TD), BF),
+            pltpu.VMEM((total, TD), BF),
+            pltpu.VMEM((FFD, total), BF),
+            pltpu.VMEM((FFD, total), BF),
+            pltpu.VMEM((FFD, total), BF),
+            pltpu.VMEM((total, FFD), BF),
+            pltpu.VMEM((GROWS, TD), F32),
+            pltpu.VMEM((GROWS, TD), BF),
+            pltpu.VMEM((NX, 2, A_PART, TD), BF),
+            pltpu.VMEM((6, A_PART, TD), BF),
+            pltpu.VMEM((2, A_PART, TD), BF),
+            pltpu.VMEM((A_PART, TD), BF),
+            pltpu.VMEM((A_PART, TD), BF),
+            pltpu.VMEM((NX * B_PART, TD), BF),
+            pltpu.VMEM((NX * B_PART, TD), BF),
+            pltpu.VMEM((NX, B_PART, TD), F32),
+            pltpu.VMEM((NX, B_PART, TD), BF),
+            pltpu.VMEM((6, B_HALF[0], TD), BF),
+            pltpu.VMEM((2, B_HALF[0], TD), BF),
+            pltpu.VMEM((2, NZ, 2, SLOTS, TD), BF),
+            pltpu.VMEM((NZ, 2, SLOTS, TD), BF),
+            pltpu.VMEM((14, SLOTS, TD), BF),
+            pltpu.VMEM((14, SLOTS, TD), BF),
+            pltpu.VMEM((SLOTS, TD), BF),
+            pltpu.VMEM((SLOTS, TD), BF),
+            pltpu.SemaphoreType.DMA((64,)),
+            pltpu.SemaphoreType.DMA((64,)),
+            pltpu.SemaphoreType.DMA((4,)),
+        ],
+        compiler_params=pltpu.CompilerParams(
+            collective_id=2, has_side_effects=True, vmem_limit_bytes=48 << 20
+        ),
+    )(rows, cots, own, turn_start, turn_len, gate_w, up_w, down_w)
+
+
 def shards(
     queries,
     keys,
@@ -393,45 +819,13 @@
     )
     rows_all = rows_all.reshape(NZ * 4 * SLOTS, TD)
     cot_all = cot_all.reshape(NZ * 4 * SLOTS, TD)
-    own_rows = own_rows.astype(F32)
-    ctx_index = lax.axis_index("ctx")
-    start = turn_start[0, ctx_index] - ctx_index * TOK
-    slot_id = jnp.arange(SLOTS, dtype=jnp.int32)[:, None]
-    place = jnp.arange(TOK, dtype=jnp.int32)[None, :]
-    packer = ((place - start == slot_id) & (slot_id < turn_len[0, ctx_index])).astype(BF)
-    contract_last = (((1,), (1,)), ((), ()))
-    contract_first = (((0,), (0,)), ((), ()))
-    gate_pre = lax.dot_general(gate_w, rows_all, contract_last, preferred_element_type=jnp.float32)
-    up_pre = lax.dot_general(up_w, rows_all, contract_last, preferred_element_type=jnp.float32)
-    sigmoid_gate = jax.nn.sigmoid(gate_pre)
-    activated = gate_pre * sigmoid_gate
-    hidden_t = (activated * up_pre).astype(jnp.bfloat16)
-    ffn_rows = lax.psum_scatter(
-        lax.dot_general(
-            hidden_t, down_w, contract_first, preferred_element_type=jnp.float32
-        ).astype(jnp.bfloat16),
-        "ctx",
-        scatter_dimension=0,
-        tiled=True,
-    ).astype(jnp.float32)
-    out_rows = (own_rows + ffn_rows).astype(jnp.bfloat16)
-    talker_out = lax.dot_general(
-        packer, out_rows, contract_first, preferred_element_type=jnp.float32
-    ).astype(jnp.bfloat16)
-    d_hidden = lax.dot_general(down_w, cot_all, contract_last, preferred_element_type=jnp.float32)
-    grad_down = jnp.dot(hidden_t, cot_all, preferred_element_type=jnp.float32)
-    d_gate = (d_hidden * up_pre * sigmoid_gate * (1.0 + gate_pre * (1.0 - sigmoid_gate))).astype(
-        jnp.bfloat16
+    talker_out, grads = talk_call(
+        rows_all, cot_all, own_rows, turn_start, turn_len, gate_w, up_w, down_w
     )
-    d_up = (d_hidden * activated).astype(jnp.bfloat16)
-    grad_gate = jnp.dot(d_gate, rows_all, preferred_element_type=jnp.float32)
-    grad_up = jnp.dot(d_up, rows_all, preferred_element_type=jnp.float32)
-    grad_gate, grad_up, grad_down = (
-        lax.psum(grad_gate.astype(jnp.bfloat16), "grp").astype(jnp.float32),
-        lax.psum(grad_up.astype(jnp.bfloat16), "grp").astype(jnp.float32),
-        lax.psum(grad_down.astype(jnp.bfloat16), "grp").astype(jnp.float32),
+    grad_down, grad_gate, grad_up = (
+        grads[n * FFD : (n + 1) * FFD].astype(F32) for n in range(3)
     )
-    return (context, talker_out[None], grad_gate, grad_up, grad_down)
+    return (context, talker_out, grad_gate, grad_up, grad_down)
 
 
 def solution(mesh):

time: 252 us -> 139 us (0.55)
  waiting for transfers between devices: 131 us -> 0 us
  Pallas kernels: 76 us -> 126 us
  between operations: 16.2 us -> 0.67 us
  matrix products: 15.1 us -> 0 us
  other arithmetic: 4.92 us -> 1.74 us
    psum x1 -> x0, waiting for transfers between devices: 108 us -> none  [shards(): lax.psum(grad_gate.astype(jnp.bfloat16), 'grp').astype(jnp.float32)]
    pallas_call x0 -> x1, Pallas kernels: none -> 49.5 us  [talk_call(): pl.pallas_call(talk_kernel, name='talk', out_shape=[jax.ShapeDtypeStruct(...]
    reduce_scatter x1 -> x0, waiting for transfers between devices: 23.1 us -> none  [shards(): lax.psum_scatter(lax.dot_general(hidden_t, down_w, contract_first, prefer...]
    dot_general x8 -> x0, matrix products: 15.1 us -> none  [the longest x1 3.31 us: shards(): lax.dot_general(hidden_t, down_w, contract_first, preferred_element_type=...]
    convert_element_type x3 -> x1, other arithmetic: 4.27 us -> 1.74 us  [shards(): grads[n * FFD:(n + 1) * FFD].astype(F32)]
    unnamed x31 -> x24, local copies, waits for them, and re-layouts: 7.53 us -> 8.64 us
  transfers between devices with their start and end apart: 2 -> 0, of which waited for: 2 -> 0; matrix products, arithmetic and copies ran while one was open for 4% -> 0% of each run, Pallas kernels for 0% -> 0%
where the time goes in v2:
time: 139 us; the launch traced here: 137 us
  Pallas kernels  126 us (91%)
  local copies, waits for them, and re-layouts  9.33 us (7%)
  other arithmetic  1.74 us (1%)
    pallas_call x1, Pallas kernels, attend_call(): pl.pallas_call(attend_kernel, name='attend', out_shape=[jax.ShapeDtypeStr...  76.2 us
    pallas_call x1, Pallas kernels, talk_call(): pl.pallas_call(talk_kernel, name='talk', out_shape=[jax.ShapeDtypeStruct(...  49.5 us
    unnamed x24, local copies, waits for them, and re-layouts  8.64 us

profile of v2, /device:TPU:2, one launch (start us, length us, event | category | flops | bytes accessed | tf_op | source)
XLA Modules:
  0.0 137.5 jit_solution(13009034278305886270)
XLA Ops:
  0.6 0.7 broadcast_in_dim.3.gain_ref
  1.3 0.0 copy-start.4
  1.3 1.0 copy-done.4
  2.3 0.0 copy-start.5
  2.3 0.9 copy-done.5
  3.3 0.0 copy-start.6
  3.3 0.8 copy-done.6
  4.1 0.0 copy-start.7
  4.1 0.8 copy-done.7
  5.0 0.0 copy-start.8
  5.0 0.7 copy-done.8
  5.6 0.0 copy-start.9
  5.6 0.7 copy-done.9
  6.3 0.7 copy-done.10
  6.9 76.2 %attend.1 = (bf16[1,128,1792]{2,1,0:T(8,128)(2,1)S(1)}, bf16[48,896]{1,0:T(8,128)(2,1)S(1)}, bf16[8,4,48,896]{3,2,1,0:T(8,128)(2,1)S(1)}, bf16[8,4,48,896]{3,2,1,0:T(8,128)(2,1)}) custom-call(bf16[1,128,1792]{2,1,0:T(8,128)(2,1)S(1)} %copy-done.4, bf16[1,128,256]{2,1,0:T(8,128)(2,1)S(1)} %copy-done.6, bf16[1,128,256]{2,1,0:T(8,128)(2,1)S(1)} %copy-done.7, ...), custom_call_target="tpu_custom_call" | custom-call | tf_op jit(solution)/shard_map/attend/pallas_call | solution.py:365
  83.1 0.0 copy-start
  83.2 1.6 %copy-done = bf16[8,4,48,896]{3,2,1,0:T(8,128)(2,1)} copy-done((bf16[8,4,48,896]{3,2,1,0:T(8,128)(2,1)}, bf16[8,4,48,896]{3,2,1,0:T(8,128)(2,1)S(1)}, u32[]{:S(2)}) %copy-start) | copy-done | bytes 2752536
  84.7 0.0 copy-done.1
  84.7 0.0 copy-done.2
  84.7 0.0 copy-done.3
  84.7 49.5 %talk.1 = (bf16[1,128,896]{2,1,0:T(8,128)(2,1)S(1)}, bf16[896,896]{1,0:T(8,128)(2,1)S(1)}) custom-call(bf16[1536,896]{1,0:T(8,128)(2,1)} %bitcast.2, bf16[1536,896]{1,0:T(8,128)(2,1)} %bitcast.3, bf16[48,896]{1,0:T(8,128)(2,1)S(1)} %get-tuple-element.14.own_ref, s32[1,32]{1,0:T(1,128)S(1)} %copy-done.8, s32[1,32]{1,0:T(1,128)S(1)} %copy-done.9, ...), custom_call_target="tpu_custom_call" | custom-call | tf_op jit(solution)/shard_map/talk/pallas_call | solution.py:758
  134.3 1.7 %slice_convert_fusion = (f32[296,896]{1,0:T(8,128)}, f32[296,896]{1,0:T(8,128)}, f32[296,896]{1,0:T(8,128)}) fusion(bf16[896,896]{1,0:T(8,128)(2,1)S(1)} %get-tuple-element.16), kind=kLoop, calls=%fused_computation | loop fusion | flops 795648 | bytes 4773888 | tf_op jit(solution)/shard_map/convert_element_type | solution.py:826
  136.0 0.8 copy.19
  136.8 0.7 copy.20
  (4 shorter events, 0.0 us)
Async XLA Ops:
  1.3 1.0 copy-start.4
  2.3 0.9 copy-start.5
  3.3 0.8 copy-start.6
  4.1 0.8 copy-start.7
  5.0 0.7 copy-start.8
  5.6 0.7 copy-start.9
  6.3 0.7 copy-start.10
  6.9 77.8 %copy-start.1 = (bf16[296,896]{1,0:T(8,128)(2,1)S(1)}, bf16[296,896]{1,0:T(8,128)(2,1)}, u32[]{:S(2)}) copy-start(bf16[296,896]{1,0:T(8,128)(2,1)} %gate_ref.1) | copy-start | bytes 1591300
  6.9 77.8 %copy-start.2 = (bf16[296,896]{1,0:T(8,128)(2,1)S(1)}, bf16[296,896]{1,0:T(8,128)(2,1)}, u32[]{:S(2)}) copy-start(bf16[296,896]{1,0:T(8,128)(2,1)} %up_ref.1) | copy-start | bytes 1591300
  6.9 77.8 %copy-start.3 = (bf16[296,896]{1,0:T(8,128)(2,1)S(1)}, bf16[296,896]{1,0:T(8,128)(2,1)}, u32[]{:S(2)}) copy-start(bf16[296,896]{1,0:T(8,128)(2,1)} %down_ref.1) | copy-start | bytes 1591300
  83.1 1.6 %copy-start = (bf16[8,4,48,896]{3,2,1,0:T(8,128)(2,1)}, bf16[8,4,48,896]{3,2,1,0:T(8,128)(2,1)S(1)}, u32[]{:S(2)}) copy-start(bf16[8,4,48,896]{3,2,1,0:T(8,128)(2,1)S(1)} %get-tuple-element.12) | copy-start | bytes 8257540

commit v3 on v2

--- a/solution.py
+++ b/solution.py
@@ -1,4 +1,3 @@
-import functools
 import math
 
 import jax
@@ -25,12 +24,15 @@
 A_PART = 64
 B_PART = 48
 B_HALF = (32, 16)
+AUX = 16
 CHUNK = 256
-AUX = 16
+KROWS = TOK + AUX
 NEG = -1e30
 MESH = pl.DeviceIdType.MESH
 BF = jnp.bfloat16
 F32 = jnp.float32
+NT = (((1,), (1,)), ((), ()))
+VMEM_LIMIT = 63 << 20
 
 
 class Net:
@@ -105,14 +107,14 @@
 
 
 class Gather:
-    def __init__(self, net, name, buf, early):
-        self.net, self.name, self.buf, self.early = net, name, buf, early
+    def __init__(self, net, name, buf, early, size):
+        self.net, self.name, self.buf, self.early, self.size = net, name, buf, early, size
 
     def slot(self, d, lane, other_core=False):
         net = self.net
         y = net.y if lane == "o" else 1 - net.y
         k = 1 - net.k if other_core else net.k
-        return self.buf.at[net.zmod(d), y * 2 + k]
+        return self.buf.at[net.zmod(d), pl.ds(pl.multiple_of((y * 2 + k) * self.size, 16), self.size)]
 
     def limit(self, way, lane):
         return 4 if (way == "+") == (lane == "o") else 3
@@ -157,8 +159,8 @@
             self.to_y(d)
         self.to_core(d, lane)
 
-    def ring(self, step):
-        for lane in ("o", "x") if self.early else ("o",):
+    def ring(self, step, lanes):
+        for lane in lanes:
             for way in ("+", "-"):
                 self.arrive(way, lane, step)
 
@@ -182,220 +184,6 @@
     return (-step, step)
 
 
-def attend_kernel(
-    q_hbm,
-    k_hbm,
-    v_hbm,
-    seg_ref,
-    start_ref,
-    len_ref,
-    w_hbm,
-    gain_ref,
-    cot_hbm,
-    ctx_ref,
-    own_ref,
-    rows_out,
-    cot_out,
-    gk,
-    gv,
-    gr,
-    gc,
-    q_raw,
-    q_buf,
-    w_buf,
-    cot_buf,
-    segq_ref,
-    bias_ref,
-    m_ref,
-    acc_ref,
-    send_sems,
-    recv_sems,
-    local_sems,
-):
-    net = Net(send_sems, recv_sems)
-    z, r = net.z, net.r
-
-    loads = [
-        pltpu.make_async_copy(k_hbm.at[0], gk.at[z, r, pl.ds(0, TOK)], local_sems.at[0]),
-        pltpu.make_async_copy(v_hbm.at[0], gv.at[z, r], local_sems.at[1]),
-        pltpu.make_async_copy(q_hbm.at[0], q_raw, local_sems.at[2]),
-        pltpu.make_async_copy(cot_hbm.at[0], cot_buf, local_sems.at[3]),
-        pltpu.make_async_copy(w_hbm, w_buf, local_sems.at[4]),
-    ]
-    for load in loads:
-        load.start()
-
-    barrier = pltpu.get_barrier_semaphore()
-    net.greet(barrier, ("+", "-", "y", "c"))
-
-    seg_row = seg_ref[...].astype(F32)
-    gk[z, r, TOK : TOK + AUX, 0:D] = jnp.broadcast_to(seg_row, (AUX, D)).astype(BF)
-    gk[z, r, TOK : TOK + AUX, D : 2 * D] = jnp.zeros((AUX, D), BF)
-
-    keys = Gather(net, "k", gk, True)
-    vals = Gather(net, "v", gv, False)
-    rows = Gather(net, "r", gr, True)
-    cots = Gather(net, "g", gc, False)
-
-    loads[0].wait()
-    loads[1].wait()
-    pl.semaphore_wait(barrier, 4)
-    keys.start()
-    vals.start()
-
-    segq_ref[...] = jnp.transpose(jnp.broadcast_to(seg_row, (TOK, D)))
-    m_ref[...] = jnp.full(m_ref.shape, NEG, F32)
-    acc_ref[...] = jnp.zeros(acc_ref.shape, F32)
-    loads[2].wait()
-    for h in range(HEADS):
-        q_buf[h] = q_raw[:, h * D : (h + 1) * D]
-
-    start = start_ref[0, net.ctx] - net.ctx * TOK
-    length = len_ref[0, net.ctx]
-    slot_id = lax.broadcasted_iota(jnp.int32, (SLOTS, TOK), 0)
-    place = lax.broadcasted_iota(jnp.int32, (SLOTS, TOK), 1)
-    packer = jnp.where((place - start == slot_id) & (slot_id < length), 1.0, 0.0).astype(BF)
-    loads[3].wait()
-    gc[z, r] = jnp.dot(packer, cot_buf[...], preferred_element_type=F32).astype(BF)
-
-    factor = math.log2(math.e) / math.sqrt(D)
-
-    def attend(d):
-        zc = net.zmod(d)
-
-        def work():
-            segq = segq_ref[...]
-            for b in range(4):
-                seg_k = gk[zc, b, TOK : TOK + AUX, 0:D].astype(F32)[0:1]
-                ok = segq == seg_k
-                if d == 0:
-                    at = (b - r) * TOK
-                    kpos = lax.broadcasted_iota(jnp.int32, (TOK, D), 1) + at
-                    qpos = lax.broadcasted_iota(jnp.int32, (TOK, D), 0)
-                    ok = ok & (kpos <= qpos)
-                bias_ref[:, b * TOK : (b + 1) * TOK] = jnp.where(ok, 0.0, NEG)
-
-            def head(i, carry):
-                for kv in range(KV_HEADS):
-                    h = i + kv * GROUP
-                    kc = gk[zc, :, 0:TOK, kv * D : (kv + 1) * D].reshape(4 * TOK, D)
-                    vc = gv[zc, :, :, kv * D : (kv + 1) * D].reshape(4 * TOK, D)
-                    vc = jnp.concatenate([vc, jnp.ones((4 * TOK, D), BF)], axis=1)
-                    s = lax.dot_general(
-                        q_buf[h], kc, (((1,), (1,)), ((), ())), preferred_element_type=F32
-                    )
-                    s = s * factor + bias_ref[...]
-                    m_old = m_ref[h]
-                    m_new = jnp.maximum(m_old, jnp.max(s, axis=1, keepdims=True))
-                    p = jnp.exp2(s - jnp.concatenate([m_new] * 4, axis=1)).astype(BF)
-                    alpha = jnp.exp2(m_old - m_new)
-                    m_ref[h] = m_new
-                    acc_ref[h] = acc_ref[h] * jnp.concatenate([alpha, alpha], axis=1) + jnp.dot(
-                        p, vc, preferred_element_type=F32
-                    )
-                return carry
-
-            lax.fori_loop(0, GROUP, head, 0)
-
-        if d == 0:
-            work()
-        else:
-            pl.when(zc < z)(work)
-
-    def attend_step(step):
-        for d in around(step):
-            keys.from_core(d)
-            vals.from_core(d)
-            attend(d)
-
-    keys.cross(0)
-    vals.crosses(0)
-    for step in range(1, 5):
-        keys.ring(step)
-        vals.ring(step)
-        if step == 4:
-            cots.start()
-        attend_step(step - 1)
-        vals.crosses(step)
-    cots.ring(1)
-    cots.crosses(0)
-    attend_step(4)
-
-    loads[4].wait()
-    for h in range(HEADS):
-        acc = acc_ref[h]
-        ctx_ref[0, :, h * D : (h + 1) * D] = (acc[:, 0:D] / acc[:, D : 2 * D]).astype(BF)
-    packed = jnp.dot(packer, ctx_ref[0], preferred_element_type=F32).astype(BF)
-    own = jnp.dot(packed, w_buf[...], preferred_element_type=F32).astype(BF)
-    own_ref[...] = own
-    own = own.astype(F32)
-    scale = lax.rsqrt(jnp.mean(own * own, axis=-1, keepdims=True) + 1e-06)
-    gr[z, r] = (own * scale * gain_ref[...]).astype(BF)
-
-    rows.start()
-    rows.cross(0)
-    cots.ring(2)
-    cots.crosses(1)
-    for step in range(1, 5):
-        rows.ring(step)
-        if step < 3:
-            cots.ring(step + 2)
-            cots.crosses(step + 1)
-    cots.crosses(4)
-    for step in range(5):
-        for d in around(step):
-            rows.from_core(d)
-            cots.from_core(d)
-    outs = [
-        pltpu.make_async_copy(gr, rows_out, local_sems.at[5]),
-        pltpu.make_async_copy(gc, cot_out, local_sems.at[6]),
-    ]
-    for out in outs:
-        out.start()
-    net.drain()
-    for out in outs:
-        out.wait()
-
-
-def attend_call(queries, keys, values, segment_ids, turn_start, turn_len, w_proj, gain, cotangent):
-    hbm = pl.BlockSpec(memory_space=pl.ANY)
-    vmem = pl.BlockSpec(memory_space=pltpu.VMEM)
-    smem = pl.BlockSpec(memory_space=pltpu.SMEM)
-    wide = (NZ, 4, SLOTS, TD)
-    return pl.pallas_call(
-        attend_kernel,
-        name="attend",
-        out_shape=[
-            jax.ShapeDtypeStruct((1, TOK, QW), BF),
-            jax.ShapeDtypeStruct((SLOTS, TD), BF),
-            jax.ShapeDtypeStruct(wide, BF),
-            jax.ShapeDtypeStruct(wide, BF),
-        ],
-        in_specs=[hbm, hbm, hbm, vmem, smem, smem, hbm, vmem, hbm],
-        out_specs=[vmem, vmem, hbm, hbm],
-        scratch_shapes=[
-            pltpu.VMEM((NZ, 4, TOK + AUX, KW), BF),
-            pltpu.VMEM((NZ, 4, TOK, KW), BF),
-            pltpu.VMEM(wide, BF),
-            pltpu.VMEM(wide, BF),
-            pltpu.VMEM((TOK, QW), BF),
-            pltpu.VMEM((HEADS, TOK, D), BF),
-            pltpu.VMEM((QW, TD), BF),
-            pltpu.VMEM((TOK, TD), BF),
-            pltpu.VMEM((TOK, D), F32),
-            pltpu.VMEM((TOK, 4 * TOK), F32),
-            pltpu.VMEM((HEADS, TOK, D), F32),
-            pltpu.VMEM((HEADS, TOK, 2 * D), F32),
-            pltpu.SemaphoreType.DMA((128,)),
-            pltpu.SemaphoreType.DMA((128,)),
-            pltpu.SemaphoreType.DMA((8,)),
-        ],
-        compiler_params=pltpu.CompilerParams(
-            collective_id=1, has_side_effects=True, vmem_limit_bytes=48 << 20
-        ),
-    )(queries, keys, values, segment_ids, turn_start, turn_len, w_proj, gain, cotangent)
-
-
 class GradSum:
     def __init__(self, net, g32, res, sa, ra, sa3, sah, rah, sb, rb, b32, sbx, rbx, sb3):
         self.net, self.g32, self.res = net, g32, res
@@ -412,12 +200,15 @@
             at, size = at + half * B_HALF[0], B_HALF[half]
         return pl.ds(pl.multiple_of(at, 16), size)
 
-    def start(self):
+    def b_send(self):
         net = self.net
         self.sb[...] = self.g32[
             pl.ds(pl.multiple_of(A_ROWS + (1 - net.h) * NX * B_PART, 16), NX * B_PART)
         ].astype(BF)
         net.send("b0", self.sb, "h", self.rb)
+
+    def a_start(self):
+        net = self.net
         for i in range(NX):
             for h in range(2):
                 at = (i * 2 + h) * A_PART
@@ -614,19 +405,44 @@
         return total + self.yr[...].astype(F32)
 
 
-def talk_kernel(
-    rows_hbm,
+def kernel(
+    q_hbm,
+    k_hbm,
+    v_hbm,
+    seg_hbm,
+    start_hbm,
+    len_hbm,
+    w_hbm,
+    gain_hbm,
+    gate_hbm,
+    up_hbm,
+    down_hbm,
     cot_hbm,
-    own_ref,
-    start_ref,
-    len_ref,
-    gate_ref,
-    up_ref,
-    down_ref,
-    out_ref,
+    ctx_out,
+    talker_out,
     grads_out,
-    rows,
-    cots,
+    gk,
+    gv,
+    gr,
+    gc,
+    q_raw,
+    q_buf,
+    ctx_buf,
+    w_buf,
+    cot_buf,
+    seg_buf,
+    start_buf,
+    len_buf,
+    gain_buf,
+    gate_w,
+    up_w,
+    down_w,
+    segq,
+    bias,
+    m_buf,
+    acc_buf,
+    own_buf,
+    out_buf,
     hid,
     d_gate,
     d_up,
@@ -655,67 +471,221 @@
     local_sems,
 ):
     net = Net(send_sems, recv_sems)
-    loads = [
-        pltpu.make_async_copy(rows_hbm, rows, local_sems.at[0]),
-        pltpu.make_async_copy(cot_hbm, cots, local_sems.at[1]),
+    z, r = net.z, net.r
+
+    def load(n, src, dst):
+        copy = pltpu.make_async_copy(src, dst, local_sems.at[n])
+        copy.start()
+        return copy
+
+    at_k = pl.ds(pl.multiple_of(r * KROWS, 16), TOK)
+    at_aux = pl.ds(pl.multiple_of(r * KROWS + TOK, 16), AUX)
+    at_v = pl.ds(pl.multiple_of(r * TOK, 16), TOK)
+    at_row = pl.ds(pl.multiple_of(r * SLOTS, 16), SLOTS)
+    load_seg = load(0, seg_hbm, seg_buf)
+    load_k = load(1, k_hbm.at[0], gk.at[z, at_k])
+    load_v = load(2, v_hbm.at[0], gv.at[z, at_v])
+    load_q = load(3, q_hbm.at[0], q_raw)
+    load_start = load(4, start_hbm, start_buf)
+    load_len = load(5, len_hbm, len_buf)
+    load_cot = load(6, cot_hbm.at[0], cot_buf)
+    load_w = load(7, w_hbm, w_buf)
+    load_gain = load(8, gain_hbm, gain_buf)
+    load_ffn = [
+        load(9, gate_hbm, gate_w),
+        load(10, up_hbm, up_w),
+        load(11, down_hbm, down_w),
     ]
-    for load in loads:
-        load.start()
+
     barrier = pltpu.get_barrier_semaphore()
     places = ("+", "-", "y", "c", "x+", "x-", "h")
     net.greet(barrier, places)
-    for load in loads:
-        load.wait()
-
-    nt = (((1,), (1,)), ((), ()))
-
-    def chunk(i, carry):
-        at = pl.ds(pl.multiple_of(i * CHUNK, CHUNK), CHUNK)
-        row = rows[at]
-        cot = cots[at]
-        gate = lax.dot_general(gate_ref[...], row, nt, preferred_element_type=F32)
-        up = lax.dot_general(up_ref[...], row, nt, preferred_element_type=F32)
-        d_hidden = lax.dot_general(down_ref[...], cot, nt, preferred_element_type=F32)
+
+    load_seg.wait()
+    seg_row = seg_buf[...].astype(F32)
+    gk[z, at_aux, 0:D] = jnp.broadcast_to(seg_row, (AUX, D)).astype(BF)
+    gk[z, at_aux, D : 2 * D] = jnp.zeros((AUX, D), BF)
+
+    keys = Gather(net, "k", gk, True, KROWS)
+    vals = Gather(net, "v", gv, False, TOK)
+    rows = Gather(net, "r", gr, True, SLOTS)
+    cots = Gather(net, "g", gc, False, SLOTS)
+
+    load_k.wait()
+    load_v.wait()
+    pl.semaphore_wait(barrier, len(places))
+    keys.start()
+    vals.start()
+
+    segq[...] = jnp.transpose(jnp.broadcast_to(seg_row, (TOK, D)))
+    m_buf[...] = jnp.full(m_buf.shape, NEG, F32)
+    acc_buf[...] = jnp.zeros(acc_buf.shape, F32)
+    load_q.wait()
+    for h in range(HEADS):
+        q_buf[h] = q_raw[:, h * D : (h + 1) * D]
+
+    load_start.wait()
+    load_len.wait()
+    start = start_buf[0, net.ctx] - net.ctx * TOK
+    length = len_buf[0, net.ctx]
+    slot_id = lax.broadcasted_iota(jnp.int32, (SLOTS, TOK), 0)
+    place = lax.broadcasted_iota(jnp.int32, (SLOTS, TOK), 1)
+    packer = jnp.where((place - start == slot_id) & (slot_id < length), 1.0, 0.0).astype(BF)
+    load_cot.wait()
+    gc[z, at_row] = jnp.dot(packer, cot_buf[...], preferred_element_type=F32).astype(BF)
+    for i in range(NZ):
+        for buf in (gr, gc):
+            buf[i, 4 * SLOTS :] = jnp.zeros((CHUNK - 4 * SLOTS, TD), BF)
+
+    factor = math.log2(math.e) / math.sqrt(D)
+
+    def attend(d):
+        zc = net.zmod(d)
+
+        def work():
+            for b in range(4):
+                aux = b * KROWS + TOK
+                ok = segq[...] == gk[zc, aux : aux + AUX, 0:D].astype(F32)[0:1]
+                if d == 0:
+                    kpos = lax.broadcasted_iota(jnp.int32, (TOK, D), 1) + (b - r) * TOK
+                    qpos = lax.broadcasted_iota(jnp.int32, (TOK, D), 0)
+                    ok = ok & (kpos <= qpos)
+                bias[:, b * TOK : (b + 1) * TOK] = jnp.where(ok, 0.0, NEG)
+
+            def head(i, carry):
+                for kv in range(KV_HEADS):
+                    h = i + kv * GROUP
+                    lanes = slice(kv * D, (kv + 1) * D)
+                    kc = jnp.concatenate(
+                        [gk[zc, b * KROWS : b * KROWS + TOK, lanes] for b in range(4)], axis=0
+                    )
+                    vc = jnp.concatenate([gv[zc, :, lanes], jnp.ones((4 * TOK, D), BF)], axis=1)
+                    s = lax.dot_general(q_buf[h], kc, NT, preferred_element_type=F32)
+                    s = s * factor + bias[...]
+                    m_old = m_buf[h]
+                    m_new = jnp.maximum(m_old, jnp.max(s, axis=1, keepdims=True))
+                    p = jnp.exp2(s - jnp.concatenate([m_new] * 4, axis=1)).astype(BF)
+                    alpha = jnp.exp2(m_old - m_new)
+                    m_buf[h] = m_new
+                    acc_buf[h] = acc_buf[h] * jnp.concatenate([alpha, alpha], axis=1) + jnp.dot(
+                        p, vc, preferred_element_type=F32
+                    )
+                return carry
+
+            lax.fori_loop(0, GROUP, head, 0)
+
+        if d == 0:
+            work()
+        else:
+            pl.when(zc < z)(work)
+
+    def attend_step(step):
+        for d in around(step):
+            keys.from_core(d)
+            vals.from_core(d)
+            attend(d)
+
+    vals.crosses(0)
+    keys.cross(0)
+    for step in range(1, 5):
+        keys.ring(step, "o")
+        vals.ring(step, "o")
+        keys.ring(step, "x")
+        if step == 3:
+            cots.start()
+        if step == 4:
+            cots.ring(1, "o")
+            cots.crosses(0)
+        attend_step(step - 1)
+        vals.crosses(step)
+    cots.ring(2, "o")
+    cots.crosses(1)
+    attend_step(4)
+
+    for h in range(HEADS):
+        acc = acc_buf[h]
+        ctx_buf[:, h * D : (h + 1) * D] = (acc[:, 0:D] / acc[:, D : 2 * D]).astype(BF)
+    load_w.wait()
+    load_gain.wait()
+    packed = jnp.dot(packer, ctx_buf[...], preferred_element_type=F32).astype(BF)
+    own = jnp.dot(packed, w_buf[...], preferred_element_type=F32).astype(BF)
+    own_buf[...] = own
+    own = own.astype(F32)
+    scale = lax.rsqrt(jnp.mean(own * own, axis=-1, keepdims=True) + 1e-06)
+    gr[z, at_row] = (own * scale * gain_buf[...]).astype(BF)
+
+    rows.start()
+    save_ctx = load(12, ctx_buf, ctx_out.at[0])
+    for wait in load_ffn:
+        wait.wait()
+
+    def ffn_in(d):
+        rows.from_core(d)
+        cots.from_core(d)
+        zc = net.zmod(d)
+        at = pl.ds(pl.multiple_of(zc * CHUNK, CHUNK), CHUNK)
+        row = gr[zc]
+        gate = lax.dot_general(gate_w[...], row, NT, preferred_element_type=F32)
+        up = lax.dot_general(up_w[...], row, NT, preferred_element_type=F32)
+        d_hidden = lax.dot_general(down_w[...], gc[zc], NT, preferred_element_type=F32)
         sig = jax.nn.sigmoid(gate)
         act = gate * sig
         hidden = act * up
         hid[:, at] = hidden.astype(BF)
-        hid_rows[at] = jnp.transpose(hidden).astype(BF)
+        hid_rows[zc] = jnp.transpose(hidden).astype(BF)
         d_gate[:, at] = (d_hidden * up * sig * (1.0 + gate * (1.0 - sig))).astype(BF)
         d_up[:, at] = (d_hidden * act).astype(BF)
-        return carry
-
-    lax.fori_loop(0, rows.shape[0] // CHUNK, chunk, 0)
-
-    for n, (left, right) in enumerate(((hid, cots), (d_gate, rows), (d_up, rows))):
-        g32[n * FFD : (n + 1) * FFD] = jnp.dot(
-            left[...], right[...], preferred_element_type=F32
-        )
-    g32[3 * FFD :] = jnp.zeros((GROWS - 3 * FFD, TD), F32)
+
+    cots.ring(3, "o")
+    cots.crosses(2)
+    rows.cross(0)
+    cots.ring(4, "o")
+    cots.crosses(3)
+    rows.ring(1, "ox")
+    ffn_in(0)
+    rows.ring(2, "ox")
+    cots.crosses(4)
+    for step in (1, 2, 3):
+        if step < 3:
+            rows.ring(step + 2, "ox")
+        for d in around(step):
+            ffn_in(d)
+    ffn_in(4)
 
     grads = GradSum(net, g32, res, sa, ra, sa3, sah, rah, sb, rb, b32, sbx, rbx, sb3)
     sums = RowSum(net, part, from_core, stage, land, ys, yr)
-    pl.semaphore_wait(barrier, len(places))
-    grads.start()
-
-    def ffn(d):
-        z = net.zmod(d)
-        at = pl.ds(pl.multiple_of(z * 4 * SLOTS, 4 * SLOTS), 4 * SLOTS)
-        total = jnp.dot(hid_rows[at], down_ref[...], preferred_element_type=F32).astype(BF)
+
+    def grad(n, left, right):
+        g32[n * FFD : (n + 1) * FFD] = jnp.dot(
+            left[...], right[...].reshape(NZ * CHUNK, TD), preferred_element_type=F32
+        )
+
+    g32[3 * FFD :] = jnp.zeros((GROWS - 3 * FFD, TD), F32)
+    grad(0, hid, gc)
+    grad(1, d_gate, gr)
+    grads.a_start()
+    grad(2, d_up, gr)
+    grads.b_send()
+
+    def ffn_out(d):
+        zc = net.zmod(d)
+        total = jnp.dot(
+            hid_rows[zc, 0 : 4 * SLOTS], down_w[...], preferred_element_type=F32
+        ).astype(BF)
         for b in range(4):
-            part[b % 2, z, b // 2] = total[b * SLOTS : (b + 1) * SLOTS]
+            part[b % 2, zc, b // 2] = total[b * SLOTS : (b + 1) * SLOTS]
         sums.swap(d)
 
     for d in (4, 3, -3):
-        ffn(d)
+        ffn_out(d)
     grads.a_pass()
     for d in (2, -2):
-        ffn(d)
+        ffn_out(d)
     for d in (4, 3, -3):
         sums.swapped(d)
     sums.step(1)
     for d in (1, -1, 0):
-        ffn(d)
+        ffn_out(d)
     grads.b_start()
     for d in (2, -2):
         sums.swapped(d)
@@ -734,94 +704,92 @@
     grads.a_forward()
     grads.b_cross()
 
-    start = start_ref[0, net.ctx] - net.ctx * TOK
-    length = len_ref[0, net.ctx]
     place = lax.broadcasted_iota(jnp.int32, (TOK, SLOTS), 0)
     slot_id = lax.broadcasted_iota(jnp.int32, (TOK, SLOTS), 1)
     spread = jnp.where((place - start == slot_id) & (slot_id < length), 1.0, 0.0).astype(BF)
-    out_rows = (own_ref[...].astype(F32) + sums.result()).astype(BF)
-    out_ref[0] = jnp.dot(spread, out_rows, preferred_element_type=F32).astype(BF)
+    out_rows = (own_buf[...].astype(F32) + sums.result()).astype(BF)
+    out_buf[...] = jnp.dot(spread, out_rows, preferred_element_type=F32).astype(BF)
+    save_out = load(13, out_buf, talker_out.at[0])
 
     grads.a_end()
     grads.b_end()
-    save = pltpu.make_async_copy(res, grads_out, local_sems.at[2])
-    save.start()
+    save_grads = load(14, res, grads_out)
     net.drain()
-    save.wait()
-
-
-def talk_call(rows, cots, own, turn_start, turn_len, gate_w, up_w, down_w):
+    for save in (save_ctx, save_out, save_grads):
+        save.wait()
+
+
+def fused(*args):
     hbm = pl.BlockSpec(memory_space=pl.ANY)
-    vmem = pl.BlockSpec(memory_space=pltpu.VMEM)
-    smem = pl.BlockSpec(memory_space=pltpu.SMEM)
-    total = NZ * 4 * SLOTS
+    scratch = (
+        ((NZ, 4 * KROWS, KW), BF),
+        ((NZ, 4 * TOK, KW), BF),
+        ((NZ, CHUNK, TD), BF),
+        ((NZ, CHUNK, TD), BF),
+        ((TOK, QW), BF),
+        ((HEADS, TOK, D), BF),
+        ((TOK, QW), BF),
+        ((QW, TD), BF),
+        ((TOK, TD), BF),
+        ((1, TOK), jnp.int32),
+        pltpu.SMEM((1, 32), jnp.int32),
+        pltpu.SMEM((1, 32), jnp.int32),
+        ((TD,), F32),
+        ((FFD, TD), BF),
+        ((FFD, TD), BF),
+        ((FFD, TD), BF),
+        ((TOK, D), F32),
+        ((TOK, 4 * TOK), F32),
+        ((HEADS, TOK, D), F32),
+        ((HEADS, TOK, 2 * D), F32),
+        ((SLOTS, TD), BF),
+        ((TOK, TD), BF),
+        ((FFD, NZ * CHUNK), BF),
+        ((FFD, NZ * CHUNK), BF),
+        ((FFD, NZ * CHUNK), BF),
+        ((NZ, CHUNK, FFD), BF),
+        ((GROWS, TD), F32),
+        ((GROWS, TD), BF),
+        ((NX, 2, A_PART, TD), BF),
+        ((6, A_PART, TD), BF),
+        ((2, A_PART, TD), BF),
+        ((A_PART, TD), BF),
+        ((A_PART, TD), BF),
+        ((NX * B_PART, TD), BF),
+        ((NX * B_PART, TD), BF),
+        ((NX, B_PART, TD), F32),
+        ((NX, B_PART, TD), BF),
+        ((6, B_HALF[0], TD), BF),
+        ((2, B_HALF[0], TD), BF),
+        ((2, NZ, 2, SLOTS, TD), BF),
+        ((NZ, 2, SLOTS, TD), BF),
+        ((14, SLOTS, TD), BF),
+        ((14, SLOTS, TD), BF),
+        ((SLOTS, TD), BF),
+        ((SLOTS, TD), BF),
+        pltpu.SemaphoreType.DMA((192,)),
+        pltpu.SemaphoreType.DMA((192,)),
+        pltpu.SemaphoreType.DMA((16,)),
+    )
     return pl.pallas_call(
-        talk_kernel,
-        name="talk",
+        kernel,
+        name="mega",
         out_shape=[
+            jax.ShapeDtypeStruct((1, TOK, QW), BF),
             jax.ShapeDtypeStruct((1, TOK, TD), BF),
             jax.ShapeDtypeStruct((GROWS, TD), BF),
         ],
-        in_specs=[hbm, hbm, vmem, smem, smem, vmem, vmem, vmem],
-        out_specs=[vmem, hbm],
-        scratch_shapes=[
-            pltpu.VMEM((total, TD), BF),
-            pltpu.VMEM((total, TD), BF),
-            pltpu.VMEM((FFD, total), BF),
-            pltpu.VMEM((FFD, total), BF),
-            pltpu.VMEM((FFD, total), BF),
-            pltpu.VMEM((total, FFD), BF),
-            pltpu.VMEM((GROWS, TD), F32),
-            pltpu.VMEM((GROWS, TD), BF),
-            pltpu.VMEM((NX, 2, A_PART, TD), BF),
-            pltpu.VMEM((6, A_PART, TD), BF),
-            pltpu.VMEM((2, A_PART, TD), BF),
-            pltpu.VMEM((A_PART, TD), BF),
-            pltpu.VMEM((A_PART, TD), BF),
-            pltpu.VMEM((NX * B_PART, TD), BF),
-            pltpu.VMEM((NX * B_PART, TD), BF),
-            pltpu.VMEM((NX, B_PART, TD), F32),
-            pltpu.VMEM((NX, B_PART, TD), BF),
-            pltpu.VMEM((6, B_HALF[0], TD), BF),
-            pltpu.VMEM((2, B_HALF[0], TD), BF),
-            pltpu.VMEM((2, NZ, 2, SLOTS, TD), BF),
-            pltpu.VMEM((NZ, 2, SLOTS, TD), BF),
-            pltpu.VMEM((14, SLOTS, TD), BF),
-            pltpu.VMEM((14, SLOTS, TD), BF),
-            pltpu.VMEM((SLOTS, TD), BF),
-            pltpu.VMEM((SLOTS, TD), BF),
-            pltpu.SemaphoreType.DMA((64,)),
-            pltpu.SemaphoreType.DMA((64,)),
-            pltpu.SemaphoreType.DMA((4,)),
-        ],
+        in_specs=[hbm] * len(args),
+        out_specs=[hbm] * 3,
+        scratch_shapes=[pltpu.VMEM(*s) if isinstance(s, tuple) else s for s in scratch],
         compiler_params=pltpu.CompilerParams(
-            collective_id=2, has_side_effects=True, vmem_limit_bytes=48 << 20
+            collective_id=1, has_side_effects=True, vmem_limit_bytes=VMEM_LIMIT
         ),
-    )(rows, cots, own, turn_start, turn_len, gate_w, up_w, down_w)
-
-
-def shards(
-    queries,
-    keys,
-    values,
-    segment_ids,
-    turn_start,
-    turn_len,
-    w_proj,
-    gain,
-    gate_w,
-    up_w,
-    down_w,
-    cotangent,
-):
-    context, own_rows, rows_all, cot_all = attend_call(
-        queries, keys, values, segment_ids, turn_start, turn_len, w_proj, gain[None], cotangent
-    )
-    rows_all = rows_all.reshape(NZ * 4 * SLOTS, TD)
-    cot_all = cot_all.reshape(NZ * 4 * SLOTS, TD)
-    talker_out, grads = talk_call(
-        rows_all, cot_all, own_rows, turn_start, turn_len, gate_w, up_w, down_w
-    )
+    )(*args)
+
+
+def shards(*args):
+    context, talker_out, grads = fused(*args)
     grad_down, grad_gate, grad_up = (
         grads[n * FFD : (n + 1) * FFD].astype(F32) for n in range(3)
     )

time: 139 us -> 125 us (0.90)
  Pallas kernels: 126 us -> 118 us
  local copies, waits for them, and re-layouts: 9.33 us -> 1.79 us
  other arithmetic: 1.74 us -> 3.16 us
    pallas_call x2 -> x1, Pallas kernels: 126 us -> 118 us  [fused(): pl.pallas_call(kernel, name='mega', out_shape=[jax.ShapeDtypeStruct((1, T...]
    unnamed x24 -> x6, local copies, waits for them, and re-layouts: 8.64 us -> 1.79 us
    convert_element_type x1, other arithmetic: 1.74 us -> 3.16 us  [shards(): grads[n * FFD:(n + 1) * FFD].astype(F32)]
where the time goes in v3:
time: 125 us; the launch traced here: 124 us
  Pallas kernels  118 us (94%)
  other arithmetic  3.16 us (3%)
  local copies, waits for them, and re-layouts  1.79 us (1%)
    pallas_call x1, Pallas kernels, fused(): pl.pallas_call(kernel, name='mega', out_shape=[jax.ShapeDtypeStruct((1, T...  118 us
    convert_element_type x1, other arithmetic, shards(): grads[n * FFD:(n + 1) * FFD].astype(F32)  3.16 us

profile of v3, /device:TPU:2, one launch (start us, length us, event | category | flops | bytes accessed | tf_op | source)
XLA Modules:
  0.0 123.8 jit_solution(6089325943394479713)
XLA Ops:
  0.6 118.2 %mega.1 = (bf16[1,128,1792]{2,1,0:T(8,128)(2,1)}, bf16[1,128,896]{2,1,0:T(8,128)(2,1)}, bf16[896,896]{1,0:T(8,128)(2,1)}) custom-call(bf16[1,128,1792]{2,1,0:T(8,128)(2,1)} %q_hbm.1, bf16[1,128,256]{2,1,0:T(8,128)(2,1)} %k_hbm.1, bf16[1,128,256]{2,1,0:T(8,128)(2,1)} %v_hbm.1, s32[1,128]{1,0:T(1,128)} %seg_hbm.1, s32[1,32]{1,0:T(1,128)} %start_hbm.1, ...), custom_call_target="tpu_custom_call" | custom-call | tf_op jit(solution)/shard_map/mega/pallas_call | solution.py:774
  118.8 0.0 copy-start
  118.8 3.2 %slice_convert_fusion = (f32[296,896]{1,0:T(8,128)}, f32[296,896]{1,0:T(8,128)}, f32[296,896]{1,0:T(8,128)}) fusion(bf16[896,896]{1,0:T(8,128)(2,1)} %get-tuple-element.10), kind=kLoop, calls=%fused_computation | loop fusion | flops 795648 | bytes 4773888 | tf_op jit(solution)/shard_map/convert_element_type | solution.py:794
  122.0 0.0 copy-start.1
  122.0 0.0 copy-done
  122.0 0.8 copy.19
  122.7 0.3 copy-done.1
  123.1 0.7 copy.20
Async XLA Ops:
  118.8 3.2 %copy-start = (bf16[1,128,1792]{2,1,0:T(8,128)(2,1)S(1)}, bf16[1,128,1792]{2,1,0:T(8,128)(2,1)}, u32[]{:S(2)}) copy-start(bf16[1,128,1792]{2,1,0:T(8,128)(2,1)} %get-tuple-element.19) | copy-start | bytes 1376260
  122.0 1.1 copy-start.1

commit v4 on v3

--- a/solution.py
+++ b/solution.py
@@ -20,10 +20,6 @@
 NX = 4
 FFD = 296
 GROWS = 896
-A_ROWS = 512
-A_PART = 64
-B_PART = 48
-B_HALF = (32, 16)
 AUX = 16
 CHUNK = 256
 KROWS = TOK + AUX
@@ -185,162 +181,164 @@
 
 
 class GradSum:
-    def __init__(self, net, g32, res, sa, ra, sa3, sah, rah, sb, rb, b32, sbx, rbx, sb3):
-        self.net, self.g32, self.res = net, g32, res
-        self.sa, self.ra, self.sa3, self.sah, self.rah = sa, ra, sa3, sah, rah
-        self.sb, self.rb, self.b32, self.sbx, self.rbx, self.sb3 = sb, rb, b32, sbx, rbx, sb3
-
-    def a_rows(self, x, h, count=1):
-        return pl.ds(pl.multiple_of((x * 2 + h) * A_PART, A_PART), count * A_PART)
-
-    def b_rows(self, h, x, half=None):
-        at = A_ROWS + (h * NX + x) * B_PART
-        size = B_PART
-        if half is not None:
-            at, size = at + half * B_HALF[0], B_HALF[half]
-        return pl.ds(pl.multiple_of(at, 16), size)
-
-    def b_send(self):
-        net = self.net
-        self.sb[...] = self.g32[
-            pl.ds(pl.multiple_of(A_ROWS + (1 - net.h) * NX * B_PART, 16), NX * B_PART)
-        ].astype(BF)
-        net.send("b0", self.sb, "h", self.rb)
-
-    def a_start(self):
-        net = self.net
+    def __init__(self, net, name, g32, res, base, size, refs):
+        self.net, self.name, self.g32, self.res = net, name, g32, res
+        self.base, self.size = base, size
+        self.refs = refs
+
+    def send(self, key, src, where, dst=None):
+        self.net.send((self.name, key), src, where, dst)
+
+    def recv(self, key, ref, where):
+        self.net.recv((self.name, key), ref, where)
+
+
+class XFirst(GradSum):
+    def rows(self, x, h):
+        return pl.ds(pl.multiple_of(self.base + (x * 2 + h) * self.size, 16), self.size)
+
+    def start(self):
+        net = self.net
+        first, land = self.refs[:2]
         for i in range(NX):
             for h in range(2):
-                at = (i * 2 + h) * A_PART
-                self.sa[i, h] = self.g32[at : at + A_PART].astype(BF)
+                at = self.base + (i * 2 + h) * self.size
+                first[i, h] = self.g32[at : at + self.size].astype(BF)
         far = net.xmod(2)
-        net.send("a1+", self.sa.at[far, 0], "x+", self.ra.at[0])
-        net.send("a1-", self.sa.at[far, 1], "x-", self.ra.at[1])
-        net.send("a2+", self.sa.at[net.xmod(1), 1], "x+", self.ra.at[2])
-        net.send("a2-", self.sa.at[net.xmod(-1), 0], "x-", self.ra.at[3])
-
-    def a_pass(self):
-        net = self.net
+        self.send("1+", first.at[far, 0], "x+", land.at[0])
+        self.send("1-", first.at[far, 1], "x-", land.at[1])
+        self.send("2+", first.at[net.xmod(1), 1], "x+", land.at[2])
+        self.send("2-", first.at[net.xmod(-1), 0], "x-", land.at[3])
+
+    def relay(self):
+        net = self.net
+        land, second = self.refs[1:3]
         for n, (way, d, half) in enumerate((("+", 1, 0), ("-", -1, 1))):
-            net.recv("a1" + way, self.ra.at[n], "x" + way)
-            own = self.g32[self.a_rows(net.xmod(d), half)]
-            self.sa3[n] = (own + self.ra[n].astype(F32)).astype(BF)
-            net.send("a3" + way, self.sa3.at[n], "x" + way, self.ra.at[4 + n])
-
-    def a_cross(self):
-        net = self.net
-        net.recv("a2+", self.ra.at[2], "x+")
-        net.recv("a2-", self.ra.at[3], "x-")
-        net.recv("a3+", self.ra.at[4], "x+")
-        net.recv("a3-", self.ra.at[5], "x-")
+            self.recv("1" + way, land.at[n], "x" + way)
+            own = self.g32[self.rows(net.xmod(d), half)]
+            second[n] = (own + land[n].astype(F32)).astype(BF)
+            self.send("3" + way, second.at[n], "x" + way, land.at[4 + n])
+
+    def cross(self):
+        net = self.net
+        land, _, over, back = self.refs[1:]
+        self.recv("2+", land.at[2], "x+")
+        self.recv("2-", land.at[3], "x-")
+        self.recv("3+", land.at[4], "x+")
+        self.recv("3-", land.at[5], "x-")
         for half, (one, two) in enumerate(((3, 4), (2, 5))):
-            rows = self.a_rows(net.x, half)
-            self.g32[rows] = self.g32[rows] + self.ra[one].astype(F32) + self.ra[two].astype(F32)
-        self.sah[...] = self.g32[self.a_rows(net.x, 1 - net.h)].astype(BF)
-        net.send("ah", self.sah, "h", self.rah)
-
-    def a_final(self):
-        net = self.net
-        net.recv("ah", self.rah, "h")
-        rows = self.a_rows(net.x, net.h)
-        self.res[rows] = (self.g32[rows] + self.rah[...].astype(F32)).astype(BF)
+            rows = self.rows(net.x, half)
+            self.g32[rows] = self.g32[rows] + land[one].astype(F32) + land[two].astype(F32)
+        over[...] = self.g32[self.rows(net.x, 1 - net.h)].astype(BF)
+        self.send("h", over, "h", back)
+
+    def final(self):
+        net = self.net
+        back = self.refs[4]
+        self.recv("h", back, "h")
+        rows = self.rows(net.x, net.h)
+        self.res[rows] = (self.g32[rows] + back[...].astype(F32)).astype(BF)
         for key, where in (("e0", "h"), ("e1+", "x+"), ("e1-", "x-")):
-            net.send(key, self.res.at[rows], where)
-
-    def a_spread(self):
-        net = self.net
-        rows = self.res.at[self.a_rows(net.x, 1 - net.h)]
-        net.recv("e0", rows, "h")
-        net.send("e2+", rows, "x+")
-        net.send("e2-", rows, "x-")
-
-    def a_forward(self):
+            self.send(key, self.res.at[rows], where)
+
+    def spread(self):
+        net = self.net
+        rows = self.res.at[self.rows(net.x, 1 - net.h)]
+        self.recv("e0", rows, "h")
+        self.send("e2+", rows, "x+")
+        self.send("e2-", rows, "x-")
+
+    def forward(self):
         net = self.net
         for way, d, half in (("+", -1, 0), ("-", 1, 1)):
             x = net.xmod(d)
-            net.recv("e1" + way, self.res.at[self.a_rows(x, net.h)], "x" + way)
-            net.recv("e2" + way, self.res.at[self.a_rows(x, 1 - net.h)], "x" + way)
-            net.send("f" + way, self.res.at[self.a_rows(x, half)], "x" + way)
-
-    def a_end(self):
+            self.recv("e1" + way, self.res.at[self.rows(x, net.h)], "x" + way)
+            self.recv("e2" + way, self.res.at[self.rows(x, 1 - net.h)], "x" + way)
+            self.send("f" + way, self.res.at[self.rows(x, half)], "x" + way)
+
+    def end(self):
         net = self.net
         for way, half in (("+", 0), ("-", 1)):
-            net.recv("f" + way, self.res.at[self.a_rows(net.xmod(2), half)], "x" + way)
-
-    def b_half(self, half):
-        return pl.ds(0 if half == 0 else B_HALF[0], B_HALF[half])
-
-    def b_start(self):
-        net = self.net
-        net.recv("b0", self.rb, "h")
+            self.recv("f" + way, self.res.at[self.rows(net.xmod(2), half)], "x" + way)
+
+
+class HFirst(GradSum):
+    def part(self, half):
+        low = self.size // 32 * 16 or self.size
+        return (0, low) if half == 0 else (low, self.size - low)
+
+    def rows(self, h, x, half=None):
+        at, size = (0, self.size) if half is None else self.part(half)
+        return pl.ds(pl.multiple_of(self.base + (h * NX + x) * self.size + at, 16), size)
+
+    def ways(self, plan):
+        return [m for m in plan if self.part(m[-1])[1]]
+
+    def start(self):
+        net = self.net
+        first, land = self.refs[:2]
+        at = self.base + (1 - net.h) * NX * self.size
+        first[...] = self.g32[pl.ds(pl.multiple_of(at, 16), NX * self.size)].astype(BF)
+        self.send("0", first, "h", land)
+
+    def cross(self):
+        net = self.net
+        back, total, second, ring = self.refs[1:5]
+        self.recv("0", back, "h")
         for i in range(NX):
-            at = slice(i * B_PART, (i + 1) * B_PART)
-            own = self.g32[self.b_rows(net.h, i)]
-            total = own + self.rb[at].astype(F32)
-            self.b32[i] = total
-            self.sbx[i] = total.astype(BF)
-        for n, (key, way, d, half) in enumerate(
-            (("b1+", "+", 2, 0), ("b1-", "-", 2, 1), ("b2+", "+", 1, 1), ("b2-", "-", -1, 0))
-        ):
-            net.send(
-                key,
-                self.sbx.at[net.xmod(d), self.b_half(half)],
-                "x" + way,
-                self.rbx.at[n, pl.ds(0, B_HALF[half])],
-            )
-
-    def b_pass(self):
-        net = self.net
-        for n, (way, d, half) in enumerate((("+", 1, 0), ("-", -1, 1))):
-            size = B_HALF[half]
-            net.recv("b1" + way, self.rbx.at[n, pl.ds(0, size)], "x" + way)
-            own = self.b32[net.xmod(d), self.b_half(half)]
-            self.sb3[n, 0:size] = (own + self.rbx[n, 0:size].astype(F32)).astype(BF)
-            net.send(
-                "b3" + way,
-                self.sb3.at[n, pl.ds(0, size)],
-                "x" + way,
-                self.rbx.at[4 + n, pl.ds(0, size)],
-            )
-
-    def b_final(self):
-        net = self.net
-        net.recv("b2+", self.rbx.at[2, pl.ds(0, B_HALF[1])], "x+")
-        net.recv("b2-", self.rbx.at[3, pl.ds(0, B_HALF[0])], "x-")
-        net.recv("b3+", self.rbx.at[4, pl.ds(0, B_HALF[0])], "x+")
-        net.recv("b3-", self.rbx.at[5, pl.ds(0, B_HALF[1])], "x-")
-        for half, (one, two) in enumerate(((3, 4), (2, 5))):
-            size = B_HALF[half]
-            total = (
-                self.b32[net.x, self.b_half(half)]
-                + self.rbx[one, 0:size].astype(F32)
-                + self.rbx[two, 0:size].astype(F32)
-            )
-            self.res[self.b_rows(net.h, net.x, half)] = total.astype(BF)
-        rows = self.res.at[self.b_rows(net.h, net.x)]
+            rows = slice(i * self.size, (i + 1) * self.size)
+            value = self.g32[self.rows(net.h, i)] + back[rows].astype(F32)
+            total[i] = value
+            second[i] = value.astype(BF)
+        plan = ((0, "1+", "+", 2, 0), (1, "1-", "-", 2, 1), (2, "2+", "+", 1, 1), (3, "2-", "-", -1, 0))
+        for n, key, way, d, half in self.ways(plan):
+            at = pl.ds(*self.part(half))
+            self.send(key, second.at[net.xmod(d), at], "x" + way, ring.at[n, at])
+
+    def relay(self):
+        net = self.net
+        total, _, ring, third = self.refs[2:]
+        for n, way, d, half in self.ways(((0, "+", 1, 0), (1, "-", -1, 1))):
+            at = pl.ds(*self.part(half))
+            self.recv("1" + way, ring.at[n, at], "x" + way)
+            third[n, at] = (total[net.xmod(d), at] + ring[n, at].astype(F32)).astype(BF)
+            self.send("3" + way, third.at[n, at], "x" + way, ring.at[4 + n, at])
+
+    def final(self):
+        net = self.net
+        total, _, ring = self.refs[2:5]
+        plan = ((2, "2+", "+", 1), (3, "2-", "-", 0), (4, "3+", "+", 0), (5, "3-", "-", 1))
+        for n, key, way, half in self.ways(plan):
+            self.recv(key, ring.at[n, pl.ds(*self.part(half))], "x" + way)
+        for one, two, half in self.ways(((3, 4, 0), (2, 5, 1))):
+            at = pl.ds(*self.part(half))
+            value = total[net.x, at] + ring[one, at].astype(F32) + ring[two, at].astype(F32)
+            self.res[self.rows(net.h, net.x, half)] = value.astype(BF)
+        rows = self.res.at[self.rows(net.h, net.x)]
         for key, where in (("q+", "x+"), ("q-", "x-"), ("p0", "h")):
-            net.send(key, rows, where)
-
-    def b_forward(self):
+            self.send(key, rows, where)
+
+    def forward(self):
         net = self.net
         for n, (way, d, half) in enumerate((("+", -1, 0), ("-", 1, 1))):
             x = net.xmod(d)
-            rows = self.res.at[self.b_rows(net.h, x)]
-            net.recv("q" + way, rows, "x" + way)
-            net.send("s" + way, self.res.at[self.b_rows(net.h, x, half)], "x" + way)
-            net.send("p%d" % (n + 1), rows, "h")
-
-    def b_cross(self):
+            rows = self.res.at[self.rows(net.h, x)]
+            self.recv("q" + way, rows, "x" + way)
+            if self.part(half)[1]:
+                self.send("s" + way, self.res.at[self.rows(net.h, x, half)], "x" + way)
+            self.send("p%d" % (n + 1), rows, "h")
+
+    def spread(self):
         net = self.net
         x = net.xmod(2)
-        for way, half in (("+", 0), ("-", 1)):
-            net.recv("s" + way, self.res.at[self.b_rows(net.h, x, half)], "x" + way)
-        net.send("p3", self.res.at[self.b_rows(net.h, x)], "h")
-
-    def b_end(self):
+        for way, half in self.ways((("+", 0), ("-", 1))):
+            self.recv("s" + way, self.res.at[self.rows(net.h, x, half)], "x" + way)
+        self.send("p3", self.res.at[self.rows(net.h, x)], "h")
+
+    def end(self):
         net = self.net
         for n, d in enumerate((0, -1, 1, 2)):
-            net.recv("p%d" % n, self.res.at[self.b_rows(1 - net.h, net.xmod(d))], "h")
+            self.recv("p%d" % n, self.res.at[self.rows(1 - net.h, net.xmod(d))], "h")
 
 
 class RowSum:
@@ -449,17 +447,10 @@
     hid_rows,
     g32,
     res,
-    sa,
-    ra,
-    sa3,
-    sah,
-    rah,
-    sb,
-    rb,
-    b32,
-    sbx,
-    rbx,
-    sb3,
+    a1_refs,
+    a2_refs,
+    b1_refs,
+    b2_refs,
     part,
     from_core,
     stage,
@@ -572,32 +563,38 @@
                     )
                 return carry
 
-            lax.fori_loop(0, GROUP, head, 0)
+            lax.fori_loop(0, GROUP, head, 0, unroll=True)
 
         if d == 0:
             work()
         else:
             pl.when(zc < z)(work)
 
+    def attend_one(d):
+        keys.from_core(d)
+        vals.from_core(d)
+        attend(d)
+
     def attend_step(step):
         for d in around(step):
-            keys.from_core(d)
-            vals.from_core(d)
-            attend(d)
+            attend_one(d)
 
     vals.crosses(0)
     keys.cross(0)
     for step in range(1, 5):
-        keys.ring(step, "o")
         vals.ring(step, "o")
-        keys.ring(step, "x")
+        keys.ring(step, "ox")
         if step == 3:
             cots.start()
         if step == 4:
             cots.ring(1, "o")
             cots.crosses(0)
-        attend_step(step - 1)
-        vals.crosses(step)
+            attend_one(-3)
+            vals.crosses(4)
+            attend_one(3)
+        else:
+            attend_step(step - 1)
+            vals.crosses(step)
     cots.ring(2, "o")
     cots.crosses(1)
     attend_step(4)
@@ -646,13 +643,16 @@
     rows.ring(2, "ox")
     cots.crosses(4)
     for step in (1, 2, 3):
+        for d in around(step):
+            ffn_in(d)
         if step < 3:
             rows.ring(step + 2, "ox")
-        for d in around(step):
-            ffn_in(d)
     ffn_in(4)
 
-    grads = GradSum(net, g32, res, sa, ra, sa3, sah, rah, sb, rb, b32, sbx, rbx, sb3)
+    a1 = XFirst(net, "a1", g32, res, 0, 32, a1_refs)
+    b1 = HFirst(net, "b1", g32, res, 256, 32, b1_refs)
+    a2 = XFirst(net, "a2", g32, res, 512, 32, a2_refs)
+    b2 = HFirst(net, "b2", g32, res, 768, 16, b2_refs)
     sums = RowSum(net, part, from_core, stage, land, ys, yr)
 
     def grad(n, left, right):
@@ -660,49 +660,59 @@
             left[...], right[...].reshape(NZ * CHUNK, TD), preferred_element_type=F32
         )
 
+    def ffn_out(*shifts):
+        for d in shifts:
+            zc = net.zmod(d)
+            total = jnp.dot(
+                hid_rows[zc, 0 : 4 * SLOTS], down_w[...], preferred_element_type=F32
+            ).astype(BF)
+            for b in range(4):
+                part[b % 2, zc, b // 2] = total[b * SLOTS : (b + 1) * SLOTS]
+            sums.swap(d)
+
+    def swapped(*shifts):
+        for d in shifts:
+            sums.swapped(d)
+
+    grad(0, hid, gc)
+    a1.start()
+    grad(1, d_gate, gr)
+    b1.start()
     g32[3 * FFD :] = jnp.zeros((GROWS - 3 * FFD, TD), F32)
-    grad(0, hid, gc)
-    grad(1, d_gate, gr)
-    grads.a_start()
     grad(2, d_up, gr)
-    grads.b_send()
-
-    def ffn_out(d):
-        zc = net.zmod(d)
-        total = jnp.dot(
-            hid_rows[zc, 0 : 4 * SLOTS], down_w[...], preferred_element_type=F32
-        ).astype(BF)
-        for b in range(4):
-            part[b % 2, zc, b // 2] = total[b * SLOTS : (b + 1) * SLOTS]
-        sums.swap(d)
-
-    for d in (4, 3, -3):
-        ffn_out(d)
-    grads.a_pass()
-    for d in (2, -2):
-        ffn_out(d)
-    for d in (4, 3, -3):
-        sums.swapped(d)
+    a2.start()
+    b2.start()
+    ffn_out(4, 3, -3)
+    a1.relay()
+    ffn_out(2, -2)
+    a2.relay()
+    swapped(4, 3, -3)
     sums.step(1)
-    for d in (1, -1, 0):
-        ffn_out(d)
-    grads.b_start()
-    for d in (2, -2):
-        sums.swapped(d)
+    a1.cross()
+    ffn_out(1, -1, 0)
+    a2.cross()
+    b1.cross()
+    swapped(2, -2)
     sums.step(2)
-    grads.a_cross()
-    for d in (1, -1, 0):
-        sums.swapped(d)
+    a1.final()
+    b2.cross()
+    b1.relay()
+    a2.final()
+    b2.relay()
+    swapped(1, -1, 0)
     sums.step(3)
-    grads.b_pass()
-    grads.a_final()
+    a1.spread()
+    b1.final()
+    a2.spread()
+    b2.final()
     sums.step(4)
-    grads.b_final()
-    grads.a_spread()
+    a1.forward()
+    b1.forward()
+    a2.forward()
+    b2.forward()
+    b1.spread()
+    b2.spread()
     sums.across()
-    grads.b_forward()
-    grads.a_forward()
-    grads.b_cross()
 
     place = lax.broadcasted_iota(jnp.int32, (TOK, SLOTS), 0)
     slot_id = lax.broadcasted_iota(jnp.int32, (TOK, SLOTS), 1)
@@ -711,12 +721,29 @@
     out_buf[...] = jnp.dot(spread, out_rows, preferred_element_type=F32).astype(BF)
     save_out = load(13, out_buf, talker_out.at[0])
 
-    grads.a_end()
-    grads.b_end()
+    for grads in (a1, a2, b1, b2):
+        grads.end()
     save_grads = load(14, res, grads_out)
     net.drain()
     for save in (save_ctx, save_out, save_grads):
         save.wait()
+
+
+def x_first(size):
+    shapes = ((NX, 2, size, TD), (6, size, TD), (2, size, TD), (size, TD), (size, TD))
+    return [pltpu.VMEM(shape, BF) for shape in shapes]
+
+
+def h_first(size):
+    wide = pltpu.VMEM((NX * size, TD), BF)
+    return [
+        wide,
+        wide,
+        pltpu.VMEM((NX, size, TD), F32),
+        pltpu.VMEM((NX, size, TD), BF),
+        pltpu.VMEM((6, size, TD), BF),
+        pltpu.VMEM((2, size, TD), BF),
+    ]
 
 
 def fused(*args):
@@ -750,25 +777,18 @@
         ((NZ, CHUNK, FFD), BF),
         ((GROWS, TD), F32),
         ((GROWS, TD), BF),
-        ((NX, 2, A_PART, TD), BF),
-        ((6, A_PART, TD), BF),
-        ((2, A_PART, TD), BF),
-        ((A_PART, TD), BF),
-        ((A_PART, TD), BF),
-        ((NX * B_PART, TD), BF),
-        ((NX * B_PART, TD), BF),
-        ((NX, B_PART, TD), F32),
-        ((NX, B_PART, TD), BF),
-        ((6, B_HALF[0], TD), BF),
-        ((2, B_HALF[0], TD), BF),
+        x_first(32),
+        x_first(32),
+        h_first(32),
+        h_first(16),
         ((2, NZ, 2, SLOTS, TD), BF),
         ((NZ, 2, SLOTS, TD), BF),
         ((14, SLOTS, TD), BF),
         ((14, SLOTS, TD), BF),
         ((SLOTS, TD), BF),
         ((SLOTS, TD), BF),
-        pltpu.SemaphoreType.DMA((192,)),
-        pltpu.SemaphoreType.DMA((192,)),
+        pltpu.SemaphoreType.DMA((256,)),
+        pltpu.SemaphoreType.DMA((256,)),
         pltpu.SemaphoreType.DMA((16,)),
     )
     return pl.pallas_call(

time: 125 us -> 108 us (0.86)
  Pallas kernels: 118 us -> 101 us
    pallas_call x1, Pallas kernels: 118 us -> 101 us  [fused(): pl.pallas_call(kernel, name='mega', out_shape=[jax.ShapeDtypeStruct((1, T...]
where the time goes in v4:
time: 108 us; the launch traced here: 107 us
  Pallas kernels  101 us (94%)
  other arithmetic  3.16 us (3%)
  local copies, waits for them, and re-layouts  1.79 us (2%)
    pallas_call x1, Pallas kernels, fused(): pl.pallas_call(kernel, name='mega', out_shape=[jax.ShapeDtypeStruct((1, T...  101 us
    convert_element_type x1, other arithmetic, shards(): grads[n * FFD:(n + 1) * FFD].astype(F32)  3.16 us

profile of v4, /device:TPU:2, one launch (start us, length us, event | category | flops | bytes accessed | tf_op | source)
XLA Modules:
  0.0 107.0 jit_solution(331232978706886330)
XLA Ops:
  0.6 101.3 %mega.1 = (bf16[1,128,1792]{2,1,0:T(8,128)(2,1)}, bf16[1,128,896]{2,1,0:T(8,128)(2,1)}, bf16[896,896]{1,0:T(8,128)(2,1)}) custom-call(bf16[1,128,1792]{2,1,0:T(8,128)(2,1)} %q_hbm.1, bf16[1,128,256]{2,1,0:T(8,128)(2,1)} %k_hbm.1, bf16[1,128,256]{2,1,0:T(8,128)(2,1)} %v_hbm.1, s32[1,128]{1,0:T(1,128)} %seg_hbm.1, s32[1,32]{1,0:T(1,128)} %start_hbm.1, ...), custom_call_target="tpu_custom_call" | custom-call | tf_op jit(solution)/shard_map/mega/pallas_call | solution.py:794
  102.0 0.0 copy-start
  102.0 3.2 %slice_convert_fusion = (f32[296,896]{1,0:T(8,128)}, f32[296,896]{1,0:T(8,128)}, f32[296,896]{1,0:T(8,128)}) fusion(bf16[896,896]{1,0:T(8,128)(2,1)} %get-tuple-element.10), kind=kLoop, calls=%fused_computation | loop fusion | flops 795648 | bytes 4773888 | tf_op jit(solution)/shard_map/convert_element_type | solution.py:814
  105.2 0.0 copy-start.1
  105.2 0.0 copy-done
  105.2 0.8 copy.19
  105.9 0.3 copy-done.1
  106.3 0.7 copy.20
Async XLA Ops:
  102.0 3.2 %copy-start = (bf16[1,128,1792]{2,1,0:T(8,128)(2,1)S(1)}, bf16[1,128,1792]{2,1,0:T(8,128)(2,1)}, u32[]{:S(2)}) copy-start(bf16[1,128,1792]{2,1,0:T(8,128)(2,1)} %get-tuple-element.19) | copy-start | bytes 1376260
  105.2 1.1 %copy-start.1 = (bf16[1,128,896]{2,1,0:T(8,128)(2,1)S(1)}, bf16[1,128,896]{2,1,0:T(8,128)(2,1)}, u32[]{:S(2)}) copy-start(bf16[1,128,896]{2,1,0:T(8,128)(2,1)} %get-tuple-element.20) | copy-start | bytes 688132

commit v5 on v4

--- a/solution.py
+++ b/solution.py
@@ -20,6 +20,7 @@
 NX = 4
 FFD = 296
 GROWS = 896
+SPLIT = 512
 AUX = 16
 CHUNK = 256
 KROWS = TOK + AUX
@@ -103,14 +104,18 @@
 
 
 class Gather:
-    def __init__(self, net, name, buf, early, size):
+    def __init__(self, net, name, buf, early, size, lanes=None):
         self.net, self.name, self.buf, self.early, self.size = net, name, buf, early, size
+        self.lanes = lanes
 
     def slot(self, d, lane, other_core=False):
         net = self.net
         y = net.y if lane == "o" else 1 - net.y
         k = 1 - net.k if other_core else net.k
-        return self.buf.at[net.zmod(d), pl.ds(pl.multiple_of((y * 2 + k) * self.size, 16), self.size)]
+        rows = pl.ds(pl.multiple_of((y * 2 + k) * self.size, 16), self.size)
+        if self.lanes is None:
+            return self.buf.at[net.zmod(d), rows]
+        return self.buf.at[net.zmod(d), rows, pl.ds(*self.lanes)]
 
     def limit(self, way, lane):
         return 4 if (way == "+") == (lane == "o") else 3
@@ -448,9 +453,10 @@
     g32,
     res,
     a1_refs,
-    a2_refs,
     b1_refs,
     b2_refs,
+    a2_refs,
+    a3_refs,
     part,
     from_core,
     stage,
@@ -499,7 +505,8 @@
 
     keys = Gather(net, "k", gk, True, KROWS)
     vals = Gather(net, "v", gv, False, TOK)
-    rows = Gather(net, "r", gr, True, SLOTS)
+    rows_a = Gather(net, "ra", gr, True, SLOTS, (0, SPLIT))
+    rows_b = Gather(net, "rb", gr, False, SLOTS, (SPLIT, TD - SPLIT))
     cots = Gather(net, "g", gc, False, SLOTS)
 
     load_k.wait()
@@ -611,13 +618,16 @@
     scale = lax.rsqrt(jnp.mean(own * own, axis=-1, keepdims=True) + 1e-06)
     gr[z, at_row] = (own * scale * gain_buf[...]).astype(BF)
 
-    rows.start()
-    save_ctx = load(12, ctx_buf, ctx_out.at[0])
+    rows_a.start()
+    rows_b.start()
+    save_ctx = load(12, ctx_buf, ctx_out)
     for wait in load_ffn:
         wait.wait()
-
-    def ffn_in(d):
-        rows.from_core(d)
+    sums = RowSum(net, part, from_core, stage, land, ys, yr)
+
+    def ffn(d):
+        rows_a.from_core(d)
+        rows_b.from_core(d)
         cots.from_core(d)
         zc = net.zmod(d)
         at = pl.ds(pl.multiple_of(zc * CHUNK, CHUNK), CHUNK)
@@ -630,98 +640,100 @@
         hidden = act * up
         hid[:, at] = hidden.astype(BF)
         hid_rows[zc] = jnp.transpose(hidden).astype(BF)
+        total = jnp.dot(
+            hid_rows[zc, 0 : 4 * SLOTS], down_w[...], preferred_element_type=F32
+        ).astype(BF)
+        for b in range(4):
+            part[b % 2, zc, b // 2] = total[b * SLOTS : (b + 1) * SLOTS]
+        sums.swap(d)
         d_gate[:, at] = (d_hidden * up * sig * (1.0 + gate * (1.0 - sig))).astype(BF)
         d_up[:, at] = (d_hidden * act).astype(BF)
 
     cots.ring(3, "o")
     cots.crosses(2)
-    rows.cross(0)
+    rows_a.cross(0)
+    rows_b.crosses(0)
     cots.ring(4, "o")
     cots.crosses(3)
-    rows.ring(1, "ox")
-    ffn_in(0)
-    rows.ring(2, "ox")
-    cots.crosses(4)
-    for step in (1, 2, 3):
-        for d in around(step):
-            ffn_in(d)
-        if step < 3:
-            rows.ring(step + 2, "ox")
-    ffn_in(4)
-
-    a1 = XFirst(net, "a1", g32, res, 0, 32, a1_refs)
-    b1 = HFirst(net, "b1", g32, res, 256, 32, b1_refs)
-    a2 = XFirst(net, "a2", g32, res, 512, 32, a2_refs)
-    b2 = HFirst(net, "b2", g32, res, 768, 16, b2_refs)
-    sums = RowSum(net, part, from_core, stage, land, ys, yr)
+    for step in range(1, 5):
+        rows_a.ring(step, "o")
+        rows_b.ring(step, "o")
+        if step > 1:
+            rows_b.crosses(step - 1)
+        rows_a.ring(step, "x")
+        if step == 2:
+            cots.crosses(4)
+        for d in around(step - 1):
+            ffn(d)
+    rows_b.crosses(4)
+    ffn(4)
 
     def grad(n, left, right):
         g32[n * FFD : (n + 1) * FFD] = jnp.dot(
             left[...], right[...].reshape(NZ * CHUNK, TD), preferred_element_type=F32
         )
 
-    def ffn_out(*shifts):
-        for d in shifts:
-            zc = net.zmod(d)
-            total = jnp.dot(
-                hid_rows[zc, 0 : 4 * SLOTS], down_w[...], preferred_element_type=F32
-            ).astype(BF)
-            for b in range(4):
-                part[b % 2, zc, b // 2] = total[b * SLOTS : (b + 1) * SLOTS]
-            sums.swap(d)
-
     def swapped(*shifts):
         for d in shifts:
             sums.swapped(d)
 
+    a1 = XFirst(net, "a1", g32, res, 0, 16, a1_refs)
+    b1 = HFirst(net, "b1", g32, res, 128, 16, b1_refs)
+    b2 = HFirst(net, "b2", g32, res, 256, 32, b2_refs)
+    a2 = XFirst(net, "a2", g32, res, 512, 32, a2_refs)
+    a3 = XFirst(net, "a3", g32, res, 768, 16, a3_refs)
+
     grad(0, hid, gc)
     a1.start()
+    b1.start()
+    swapped(4, 3, -3)
+    sums.step(1)
     grad(1, d_gate, gr)
-    b1.start()
+    b2.start()
     g32[3 * FFD :] = jnp.zeros((GROWS - 3 * FFD, TD), F32)
     grad(2, d_up, gr)
     a2.start()
-    b2.start()
-    ffn_out(4, 3, -3)
+    a3.start()
     a1.relay()
-    ffn_out(2, -2)
-    a2.relay()
-    swapped(4, 3, -3)
-    sums.step(1)
-    a1.cross()
-    ffn_out(1, -1, 0)
-    a2.cross()
-    b1.cross()
     swapped(2, -2)
     sums.step(2)
+    b1.cross()
+    a1.cross()
+    a2.relay()
+    a3.relay()
+    b1.relay()
+    a3.cross()
+    a2.cross()
+    swapped(1, -1, 0)
+    sums.step(3)
     a1.final()
     b2.cross()
-    b1.relay()
+    b1.final()
+    a3.final()
     a2.final()
     b2.relay()
-    swapped(1, -1, 0)
-    sums.step(3)
+    sums.step(4)
     a1.spread()
-    b1.final()
+    b1.forward()
+    a1.forward()
+    b2.final()
+    b1.spread()
+    a3.spread()
     a2.spread()
-    b2.final()
-    sums.step(4)
-    a1.forward()
-    b1.forward()
+    sums.across()
+    a3.forward()
+    b2.forward()
     a2.forward()
-    b2.forward()
-    b1.spread()
     b2.spread()
-    sums.across()
 
     place = lax.broadcasted_iota(jnp.int32, (TOK, SLOTS), 0)
     slot_id = lax.broadcasted_iota(jnp.int32, (TOK, SLOTS), 1)
     spread = jnp.where((place - start == slot_id) & (slot_id < length), 1.0, 0.0).astype(BF)
     out_rows = (own_buf[...].astype(F32) + sums.result()).astype(BF)
     out_buf[...] = jnp.dot(spread, out_rows, preferred_element_type=F32).astype(BF)
-    save_out = load(13, out_buf, talker_out.at[0])
-
-    for grads in (a1, a2, b1, b2):
+    save_out = load(13, out_buf, talker_out)
+
+    for grads in (a1, b1, a3, a2, b2):
         grads.end()
     save_grads = load(14, res, grads_out)
     net.drain()
@@ -777,26 +789,27 @@
         ((NZ, CHUNK, FFD), BF),
         ((GROWS, TD), F32),
         ((GROWS, TD), BF),
+        x_first(16),
+        h_first(16),
+        h_first(32),
         x_first(32),
-        x_first(32),
-        h_first(32),
-        h_first(16),
+        x_first(16),
         ((2, NZ, 2, SLOTS, TD), BF),
         ((NZ, 2, SLOTS, TD), BF),
         ((14, SLOTS, TD), BF),
         ((14, SLOTS, TD), BF),
         ((SLOTS, TD), BF),
         ((SLOTS, TD), BF),
-        pltpu.SemaphoreType.DMA((256,)),
-        pltpu.SemaphoreType.DMA((256,)),
+        pltpu.SemaphoreType.DMA((288,)),
+        pltpu.SemaphoreType.DMA((288,)),
         pltpu.SemaphoreType.DMA((16,)),
     )
     return pl.pallas_call(
         kernel,
         name="mega",
         out_shape=[
-            jax.ShapeDtypeStruct((1, TOK, QW), BF),
-            jax.ShapeDtypeStruct((1, TOK, TD), BF),
+            jax.ShapeDtypeStruct((TOK, QW), BF),
+            jax.ShapeDtypeStruct((TOK, TD), BF),
             jax.ShapeDtypeStruct((GROWS, TD), BF),
         ],
         in_specs=[hbm] * len(args),
@@ -808,12 +821,56 @@
     )(*args)
 
 
+def finish_kernel(ctx_in, talker_in, grads_in, ctx_out, talker_out, down_out, gate_out, up_out, low, wide, sems):
+    def move(n, src, dst):
+        copy = pltpu.make_async_copy(src, dst, sems.at[n])
+        copy.start()
+        return copy
+
+    step = 128
+    loads = [
+        move(n, grads_in.at[pl.ds(n * step, step)], low.at[pl.ds(n * step, step)])
+        for n in range(GROWS // step)
+    ]
+    moves = [move(7, ctx_in, ctx_out.at[0]), move(8, talker_in, talker_out.at[0])]
+    outs = [down_out, gate_out, up_out]
+    for n, load in enumerate(loads):
+        load.wait()
+        wide[n * step : (n + 1) * step] = low[n * step : (n + 1) * step].astype(F32)
+        done = 3 - len(outs)
+        if outs and (n + 1) * step >= (done + 1) * FFD:
+            moves.append(move(9 + done, wide.at[pl.ds(done * FFD, FFD)], outs.pop(0)))
+    for copy in moves:
+        copy.wait()
+
+
+def finish(context, talker, grads):
+    hbm = pl.BlockSpec(memory_space=pl.ANY)
+    grad = jax.ShapeDtypeStruct((FFD, TD), F32)
+    return pl.pallas_call(
+        finish_kernel,
+        name="finish",
+        out_shape=[
+            jax.ShapeDtypeStruct((1, TOK, QW), BF),
+            jax.ShapeDtypeStruct((1, TOK, TD), BF),
+            grad,
+            grad,
+            grad,
+        ],
+        in_specs=[hbm] * 3,
+        out_specs=[hbm] * 5,
+        scratch_shapes=[
+            pltpu.VMEM((GROWS, TD), BF),
+            pltpu.VMEM((GROWS, TD), F32),
+            pltpu.SemaphoreType.DMA((12,)),
+        ],
+        compiler_params=pltpu.CompilerParams(vmem_limit_bytes=VMEM_LIMIT),
+    )(context, talker, grads)
+
+
 def shards(*args):
-    context, talker_out, grads = fused(*args)
-    grad_down, grad_gate, grad_up = (
-        grads[n * FFD : (n + 1) * FFD].astype(F32) for n in range(3)
-    )
-    return (context, talker_out, grad_gate, grad_up, grad_down)
+    context, talker, grad_down, grad_gate, grad_up = finish(*fused(*args))
+    return (context, talker, grad_gate, grad_up, grad_down)
 
 
 def solution(mesh):

time: 108 us -> 132 us (1.22)
  Pallas kernels: 101 us -> 129 us
  other arithmetic: 3.16 us -> 0 us
  local copies, waits for them, and re-layouts: 1.79 us -> 0 us
    pallas_call x1 -> x2, Pallas kernels: 101 us -> 129 us  [the longest x1 107 us: fused(): pl.pallas_call(kernel, name='mega', out_shape=[jax.ShapeDtypeStruct((TOK,...]
    convert_element_type x1 -> x0, other arithmetic: 3.16 us -> none  [shards(): grads[n * FFD:(n + 1) * FFD].astype(F32)]
    unnamed x6 -> x0, local copies, waits for them, and re-layouts: 1.79 us -> none
where the time goes in v5:
time: 132 us; the launch traced here: 130 us
  Pallas kernels  129 us (98%)
    pallas_call x1, Pallas kernels, fused(): pl.pallas_call(kernel, name='mega', out_shape=[jax.ShapeDtypeStruct((TOK,...  107 us
    pallas_call x1, Pallas kernels, finish(): pl.pallas_call(finish_kernel, name='finish', out_shape=[jax.ShapeDtypeStr...  22.1 us

profile of v5, /device:TPU:2, one launch (start us, length us, event | category | flops | bytes accessed | tf_op | source)
XLA Modules:
  0.0 129.7 jit_solution(7883852076144644595)
XLA Ops:
  0.6 106.8 %mega.1 = (bf16[128,1792]{1,0:T(8,128)(2,1)}, bf16[128,896]{1,0:T(8,128)(2,1)}, bf16[896,896]{1,0:T(8,128)(2,1)}) custom-call(bf16[1,128,1792]{2,1,0:T(8,128)(2,1)} %q_hbm.1, bf16[1,128,256]{2,1,0:T(8,128)(2,1)} %k_hbm.1, bf16[1,128,256]{2,1,0:T(8,128)(2,1)} %v_hbm.1, s32[1,128]{1,0:T(1,128)} %seg_hbm.1, s32[1,32]{1,0:T(1,128)} %start_hbm.1, ...), custom_call_target="tpu_custom_call" | custom-call | tf_op jit(solution)/shard_map/mega/pallas_call | solution.py:807
  107.5 22.1 %finish.1 = (bf16[1,128,1792]{2,1,0:T(8,128)(2,1)}, bf16[1,128,896]{2,1,0:T(8,128)(2,1)}, f32[296,896]{1,0:T(8,128)}, f32[296,896]{1,0:T(8,128)}, f32[296,896]{1,0:T(8,128)}) custom-call(bf16[128,1792]{1,0:T(8,128)(2,1)} %get-tuple-element.13.ctx_in, bf16[128,896]{1,0:T(8,128)(2,1)} %get-tuple-element.14.talker_in, bf16[896,896]{1,0:T(8,128)(2,1)} %get-tuple-element.15.grads_in), custom_call_target="tpu_custom_call" | custom-call | tf_op jit(solution)/shard_map/finish/pallas_call | solution.py:850

commit v6 on v4

--- a/solution.py
+++ b/solution.py
@@ -46,6 +46,7 @@
         self.recv_sems = recv_sems
         self.ids = {}
         self.sent = []
+        self.older = []
 
     def zmod(self, d):
         return lax.rem(self.z + d + NZ, NZ)
@@ -96,10 +97,14 @@
     def recv(self, key, ref, where):
         self.copy(key, ref, ref, where).wait_recv()
 
+    def settle(self):
+        for copy in self.older:
+            copy.wait_send()
+        self.older, self.sent = self.sent, []
+
     def drain(self):
-        for copy in self.sent:
-            copy.wait_send()
-        self.sent = []
+        self.settle()
+        self.settle()
 
 
 class Gather:
@@ -277,23 +282,38 @@
     def start(self):
         net = self.net
         first, land = self.refs[:2]
-        at = self.base + (1 - net.h) * NX * self.size
-        first[...] = self.g32[pl.ds(pl.multiple_of(at, 16), NX * self.size)].astype(BF)
-        self.send("0", first, "h", land)
+        for i in range(NX):
+            first[i] = self.g32[self.rows(1 - net.h, i)].astype(BF)
+        for d in (2, 1, -1, 0):
+            x = net.xmod(d)
+            self.send(("0", d), first.at[x], "h", land.at[x])
+
+    def pair(self, d):
+        net = self.net
+        back, total, second = self.refs[1:4]
+        x = net.xmod(d)
+        self.recv(("0", d), back.at[x], "h")
+        value = self.g32[self.rows(net.h, x)] + back[x].astype(F32)
+        total[x] = value
+        second[x] = value.astype(BF)
+
+    def pass_on(self, n, key, way, d, half):
+        second, ring = self.refs[3:5]
+        if self.part(half)[1]:
+            at = pl.ds(*self.part(half))
+            self.send(key, second.at[self.net.xmod(d), at], "x" + way, ring.at[n, at])
+
+    def cross_far(self):
+        self.pair(2)
+        self.pass_on(0, "1+", "+", 2, 0)
+        self.pass_on(1, "1-", "-", 2, 1)
 
     def cross(self):
-        net = self.net
-        back, total, second, ring = self.refs[1:5]
-        self.recv("0", back, "h")
-        for i in range(NX):
-            rows = slice(i * self.size, (i + 1) * self.size)
-            value = self.g32[self.rows(net.h, i)] + back[rows].astype(F32)
-            total[i] = value
-            second[i] = value.astype(BF)
-        plan = ((0, "1+", "+", 2, 0), (1, "1-", "-", 2, 1), (2, "2+", "+", 1, 1), (3, "2-", "-", -1, 0))
-        for n, key, way, d, half in self.ways(plan):
-            at = pl.ds(*self.part(half))
-            self.send(key, second.at[net.xmod(d), at], "x" + way, ring.at[n, at])
+        self.pair(1)
+        self.pass_on(2, "2+", "+", 1, 1)
+        self.pair(-1)
+        self.pass_on(3, "2-", "-", -1, 0)
+        self.pair(0)
 
     def relay(self):
         net = self.net
@@ -595,6 +615,7 @@
         else:
             attend_step(step - 1)
             vals.crosses(step)
+        net.settle()
     cots.ring(2, "o")
     cots.crosses(1)
     attend_step(4)
@@ -612,7 +633,7 @@
     gr[z, at_row] = (own * scale * gain_buf[...]).astype(BF)
 
     rows.start()
-    save_ctx = load(12, ctx_buf, ctx_out.at[0])
+    save_ctx = load(12, ctx_buf, ctx_out)
     for wait in load_ffn:
         wait.wait()
 
@@ -638,27 +659,7 @@
     rows.cross(0)
     cots.ring(4, "o")
     cots.crosses(3)
-    rows.ring(1, "ox")
-    ffn_in(0)
-    rows.ring(2, "ox")
-    cots.crosses(4)
-    for step in (1, 2, 3):
-        for d in around(step):
-            ffn_in(d)
-        if step < 3:
-            rows.ring(step + 2, "ox")
-    ffn_in(4)
-
-    a1 = XFirst(net, "a1", g32, res, 0, 32, a1_refs)
-    b1 = HFirst(net, "b1", g32, res, 256, 32, b1_refs)
-    a2 = XFirst(net, "a2", g32, res, 512, 32, a2_refs)
-    b2 = HFirst(net, "b2", g32, res, 768, 16, b2_refs)
     sums = RowSum(net, part, from_core, stage, land, ys, yr)
-
-    def grad(n, left, right):
-        g32[n * FFD : (n + 1) * FFD] = jnp.dot(
-            left[...], right[...].reshape(NZ * CHUNK, TD), preferred_element_type=F32
-        )
 
     def ffn_out(*shifts):
         for d in shifts:
@@ -670,58 +671,91 @@
                 part[b % 2, zc, b // 2] = total[b * SLOTS : (b + 1) * SLOTS]
             sums.swap(d)
 
+    rows.ring(1, "ox")
+    ffn_in(0)
+    ffn_out(0)
+    net.settle()
+    rows.ring(2, "ox")
+    cots.crosses(4)
+    ffn_in(-1)
+    ffn_in(1)
+    ffn_out(-1, 1)
+    net.settle()
+    rows.ring(3, "ox")
+    ffn_in(-2)
+    ffn_in(2)
+    net.settle()
+    rows.ring(4, "ox")
+    ffn_in(-3)
+    ffn_in(3)
+    ffn_in(4)
+
+    b1 = HFirst(net, "b1", g32, res, 0, 32, b1_refs)
+    a1 = XFirst(net, "a1", g32, res, 256, 32, a1_refs)
+    a2 = XFirst(net, "a2", g32, res, 512, 32, a2_refs)
+    b2 = HFirst(net, "b2", g32, res, 768, 16, b2_refs)
+
+    def grad(n, left, right):
+        g32[n * FFD : (n + 1) * FFD] = jnp.dot(
+            left[...], right[...].reshape(NZ * CHUNK, TD), preferred_element_type=F32
+        )
+
     def swapped(*shifts):
         for d in shifts:
             sums.swapped(d)
 
     grad(0, hid, gc)
+    b1.start()
+    grad(1, d_gate, gr)
     a1.start()
-    grad(1, d_gate, gr)
-    b1.start()
     g32[3 * FFD :] = jnp.zeros((GROWS - 3 * FFD, TD), F32)
     grad(2, d_up, gr)
     a2.start()
     b2.start()
     ffn_out(4, 3, -3)
+    b1.cross_far()
     a1.relay()
     ffn_out(2, -2)
     a2.relay()
     swapped(4, 3, -3)
     sums.step(1)
+    b1.cross()
+    b2.cross_far()
     a1.cross()
-    ffn_out(1, -1, 0)
+    b1.relay()
+    b2.cross()
     a2.cross()
-    b1.cross()
     swapped(2, -2)
     sums.step(2)
+    net.settle()
+    b2.relay()
+    b1.final()
     a1.final()
-    b2.cross()
-    b1.relay()
-    a2.final()
-    b2.relay()
     swapped(1, -1, 0)
     sums.step(3)
+    b1.forward()
+    a2.final()
+    b2.final()
+    net.settle()
     a1.spread()
-    b1.final()
+    b1.spread()
+    b2.forward()
+    sums.step(4)
     a2.spread()
-    b2.final()
-    sums.step(4)
     a1.forward()
-    b1.forward()
+    b2.spread()
     a2.forward()
-    b2.forward()
-    b1.spread()
-    b2.spread()
     sums.across()
+    net.settle()
 
     place = lax.broadcasted_iota(jnp.int32, (TOK, SLOTS), 0)
     slot_id = lax.broadcasted_iota(jnp.int32, (TOK, SLOTS), 1)
     spread = jnp.where((place - start == slot_id) & (slot_id < length), 1.0, 0.0).astype(BF)
     out_rows = (own_buf[...].astype(F32) + sums.result()).astype(BF)
     out_buf[...] = jnp.dot(spread, out_rows, preferred_element_type=F32).astype(BF)
-    save_out = load(13, out_buf, talker_out.at[0])
-
-    for grads in (a1, a2, b1, b2):
+    save_out = load(13, out_buf, talker_out)
+
+    for grads in (b1, a1, b2, a2):
         grads.end()
     save_grads = load(14, res, grads_out)
     net.drain()
@@ -735,12 +769,12 @@
 
 
 def h_first(size):
-    wide = pltpu.VMEM((NX * size, TD), BF)
+    piece = pltpu.VMEM((NX, size, TD), BF)
     return [
-        wide,
-        wide,
+        piece,
+        piece,
         pltpu.VMEM((NX, size, TD), F32),
-        pltpu.VMEM((NX, size, TD), BF),
+        piece,
         pltpu.VMEM((6, size, TD), BF),
         pltpu.VMEM((2, size, TD), BF),
     ]
@@ -795,8 +829,8 @@
         kernel,
         name="mega",
         out_shape=[
-            jax.ShapeDtypeStruct((1, TOK, QW), BF),
-            jax.ShapeDtypeStruct((1, TOK, TD), BF),
+            jax.ShapeDtypeStruct((TOK, QW), BF),
+            jax.ShapeDtypeStruct((TOK, TD), BF),
             jax.ShapeDtypeStruct((GROWS, TD), BF),
         ],
         in_specs=[hbm] * len(args),
@@ -808,12 +842,65 @@
     )(*args)
 
 
+def finish_kernel(ctx_in, talker_in, grads_in, ctx_out, talker_out, down_out, gate_out, up_out, low, wide, ctx_buf, talker_buf, sems):
+    def move(n, src, dst):
+        copy = pltpu.make_async_copy(src, dst, sems.at[n])
+        copy.start()
+        return copy
+
+    step = 128
+    loads = [
+        move(n, grads_in.at[pl.ds(n * step, step)], low.at[pl.ds(n * step, step)])
+        for n in range(GROWS // step)
+    ]
+    hops = [
+        (move(7, ctx_in, ctx_buf), 12, ctx_buf, ctx_out.at[0]),
+        (move(8, talker_in, talker_buf), 13, talker_buf, talker_out.at[0]),
+    ]
+    moves = []
+    for hop, n, src, dst in hops:
+        hop.wait()
+        moves.append(move(n, src, dst))
+    outs = [down_out, gate_out, up_out]
+    for n, load in enumerate(loads):
+        load.wait()
+        wide[n * step : (n + 1) * step] = low[n * step : (n + 1) * step].astype(F32)
+        done = 3 - len(outs)
+        if outs and (n + 1) * step >= (done + 1) * FFD:
+            moves.append(move(9 + done, wide.at[pl.ds(done * FFD, FFD)], outs.pop(0)))
+    for copy in moves:
+        copy.wait()
+
+
+def finish(context, talker, grads):
+    hbm = pl.BlockSpec(memory_space=pl.ANY)
+    grad = jax.ShapeDtypeStruct((FFD, TD), F32)
+    return pl.pallas_call(
+        finish_kernel,
+        name="finish",
+        out_shape=[
+            jax.ShapeDtypeStruct((1, TOK, QW), BF),
+            jax.ShapeDtypeStruct((1, TOK, TD), BF),
+            grad,
+            grad,
+            grad,
+        ],
+        in_specs=[hbm] * 3,
+        out_specs=[hbm] * 5,
+        scratch_shapes=[
+            pltpu.VMEM((GROWS, TD), BF),
+            pltpu.VMEM((GROWS, TD), F32),
+            pltpu.VMEM((TOK, QW), BF),
+            pltpu.VMEM((TOK, TD), BF),
+            pltpu.SemaphoreType.DMA((16,)),
+        ],
+        compiler_params=pltpu.CompilerParams(vmem_limit_bytes=VMEM_LIMIT),
+    )(context, talker, grads)
+
+
 def shards(*args):
-    context, talker_out, grads = fused(*args)
-    grad_down, grad_gate, grad_up = (
-        grads[n * FFD : (n + 1) * FFD].astype(F32) for n in range(3)
-    )
-    return (context, talker_out, grad_gate, grad_up, grad_down)
+    context, talker, grad_down, grad_gate, grad_up = finish(*fused(*args))
+    return (context, talker, grad_gate, grad_up, grad_down)
 
 
 def solution(mesh):

time: 108 us -> 106 us (0.981); the launches traced: 107 us -> 106 us
  Pallas kernels: 101 us -> 105 us
  other arithmetic: 3.16 us -> 0 us
  local copies, waits for them, and re-layouts: 1.79 us -> 0 us
    pallas_call x1 -> x2, Pallas kernels: 101 us -> 105 us  [the longest x1 102 us: fused(): pl.pallas_call(kernel, name='mega', out_shape=[jax.ShapeDtypeStruct((TOK,...]
    convert_element_type x1 -> x0, other arithmetic: 3.16 us -> none  [shards(): grads[n * FFD:(n + 1) * FFD].astype(F32)]
    unnamed x6 -> x0, local copies, waits for them, and re-layouts: 1.79 us -> none
where the time goes in v6:
time: 106 us
  Pallas kernels  105 us (99%)
    pallas_call x1, Pallas kernels, fused(): pl.pallas_call(kernel, name='mega', out_shape=[jax.ShapeDtypeStruct((TOK,...  102 us
    pallas_call x1, Pallas kernels, finish(): pl.pallas_call(finish_kernel, name='finish', out_shape=[jax.ShapeDtypeStr...  3.68 us

profile of v6, /device:TPU:2, one launch (start us, length us, event | category | flops | bytes accessed | tf_op | source)
XLA Modules:
  0.0 106.2 jit_solution(797654174988243677)
XLA Ops:
  0.6 101.7 %mega.1 = (bf16[128,1792]{1,0:T(8,128)(2,1)}, bf16[128,896]{1,0:T(8,128)(2,1)}, bf16[896,896]{1,0:T(8,128)(2,1)}) custom-call(bf16[1,128,1792]{2,1,0:T(8,128)(2,1)} %q_hbm.1, bf16[1,128,256]{2,1,0:T(8,128)(2,1)} %k_hbm.1, bf16[1,128,256]{2,1,0:T(8,128)(2,1)} %v_hbm.1, s32[1,128]{1,0:T(1,128)} %seg_hbm.1, s32[1,32]{1,0:T(1,128)} %start_hbm.1, ...), custom_call_target="tpu_custom_call" | custom-call | tf_op jit(solution)/shard_map/mega/pallas_call | solution.py:828
  102.3 3.7 %finish.1 = (bf16[1,128,1792]{2,1,0:T(8,128)(2,1)}, bf16[1,128,896]{2,1,0:T(8,128)(2,1)}, f32[296,896]{1,0:T(8,128)}, f32[296,896]{1,0:T(8,128)}, f32[296,896]{1,0:T(8,128)}) custom-call(bf16[128,1792]{1,0:T(8,128)(2,1)} %get-tuple-element.13.ctx_in, bf16[128,896]{1,0:T(8,128)(2,1)} %get-tuple-element.14.talker_in, bf16[896,896]{1,0:T(8,128)(2,1)} %get-tuple-element.15.grads_in), custom_call_target="tpu_custom_call" | custom-call | tf_op jit(solution)/shard_map/finish/pallas_call | solution.py:878

commit v7 on v6

--- a/solution.py
+++ b/solution.py
@@ -467,10 +467,11 @@
     hid_rows,
     g32,
     res,
+    b1_refs,
     a1_refs,
     a2_refs,
-    b1_refs,
     b2_refs,
+    a3_refs,
     part,
     from_core,
     stage,
@@ -684,6 +685,7 @@
     rows.ring(3, "ox")
     ffn_in(-2)
     ffn_in(2)
+    ffn_out(-2, 2)
     net.settle()
     rows.ring(4, "ox")
     ffn_in(-3)
@@ -692,8 +694,9 @@
 
     b1 = HFirst(net, "b1", g32, res, 0, 32, b1_refs)
     a1 = XFirst(net, "a1", g32, res, 256, 32, a1_refs)
-    a2 = XFirst(net, "a2", g32, res, 512, 32, a2_refs)
-    b2 = HFirst(net, "b2", g32, res, 768, 16, b2_refs)
+    a2 = XFirst(net, "a2", g32, res, 512, 16, a2_refs)
+    b2 = HFirst(net, "b2", g32, res, 640, 16, b2_refs)
+    a3 = XFirst(net, "a3", g32, res, 768, 16, a3_refs)
 
     def grad(n, left, right):
         g32[n * FFD : (n + 1) * FFD] = jnp.dot(
@@ -706,47 +709,52 @@
 
     grad(0, hid, gc)
     b1.start()
+    ffn_out(4, 3, -3)
     grad(1, d_gate, gr)
     a1.start()
+    swapped(4, 3, -3)
+    sums.step(1)
     g32[3 * FFD :] = jnp.zeros((GROWS - 3 * FFD, TD), F32)
     grad(2, d_up, gr)
+    b2.start()
     a2.start()
-    b2.start()
-    ffn_out(4, 3, -3)
+    a3.start()
     b1.cross_far()
     a1.relay()
-    ffn_out(2, -2)
+    swapped(2, -2)
+    sums.step(2)
     a2.relay()
-    swapped(4, 3, -3)
-    sums.step(1)
+    a3.relay()
     b1.cross()
+    net.settle()
+    b1.relay()
     b2.cross_far()
     a1.cross()
-    b1.relay()
+    a2.cross()
+    a3.cross()
     b2.cross()
-    a2.cross()
-    swapped(2, -2)
-    sums.step(2)
-    net.settle()
     b2.relay()
-    b1.final()
-    a1.final()
     swapped(1, -1, 0)
     sums.step(3)
+    b1.final()
+    net.settle()
+    a1.final()
+    b2.final()
+    a2.final()
+    a3.final()
     b1.forward()
-    a2.final()
-    b2.final()
-    net.settle()
+    sums.step(4)
+    b2.forward()
     a1.spread()
+    a2.spread()
+    a3.spread()
     b1.spread()
-    b2.forward()
-    sums.step(4)
-    a2.spread()
-    a1.forward()
     b2.spread()
-    a2.forward()
     sums.across()
     net.settle()
+    a2.forward()
+    a3.forward()
+    a1.forward()
 
     place = lax.broadcasted_iota(jnp.int32, (TOK, SLOTS), 0)
     slot_id = lax.broadcasted_iota(jnp.int32, (TOK, SLOTS), 1)
@@ -755,11 +763,13 @@
     out_buf[...] = jnp.dot(spread, out_rows, preferred_element_type=F32).astype(BF)
     save_out = load(13, out_buf, talker_out)
 
-    for grads in (b1, a1, b2, a2):
+    saves = [save_ctx, save_out]
+    for n, grads in enumerate((b1, b2, a2, a3, a1)):
         grads.end()
-    save_grads = load(14, res, grads_out)
+        at = pl.ds(grads.base, 8 * grads.size)
+        saves.append(load(14 + n, res.at[at], grads_out.at[at]))
     net.drain()
-    for save in (save_ctx, save_out, save_grads):
+    for save in saves:
         save.wait()
 
 
@@ -811,10 +821,11 @@
         ((NZ, CHUNK, FFD), BF),
         ((GROWS, TD), F32),
         ((GROWS, TD), BF),
+        h_first(32),
         x_first(32),
-        x_first(32),
-        h_first(32),
+        x_first(16),
         h_first(16),
+        x_first(16),
         ((2, NZ, 2, SLOTS, TD), BF),
         ((NZ, 2, SLOTS, TD), BF),
         ((14, SLOTS, TD), BF),
@@ -823,7 +834,7 @@
         ((SLOTS, TD), BF),
         pltpu.SemaphoreType.DMA((256,)),
         pltpu.SemaphoreType.DMA((256,)),
-        pltpu.SemaphoreType.DMA((16,)),
+        pltpu.SemaphoreType.DMA((24,)),
     )
     return pl.pallas_call(
         kernel,

time: 106 us -> 104 us (0.981)
  Pallas kernels: 105 us -> 103 us
    pallas_call x1, Pallas kernels: 102 us -> 99.4 us  [fused(): pl.pallas_call(kernel, name='mega', out_shape=[jax.ShapeDtypeStruct((TOK,...]
where the time goes in v7:
time: 104 us
  Pallas kernels  103 us (99%)
    pallas_call x1, Pallas kernels, fused(): pl.pallas_call(kernel, name='mega', out_shape=[jax.ShapeDtypeStruct((TOK,...  99.4 us
    pallas_call x1, Pallas kernels, finish(): pl.pallas_call(finish_kernel, name='finish', out_shape=[jax.ShapeDtypeStr...  3.68 us

profile of v7, /device:TPU:2, one launch (start us, length us, event | category | flops | bytes accessed | tf_op | source)
XLA Modules:
  0.0 103.9 jit_solution(6047232498799064470)
XLA Ops:
  0.6 99.4 %mega.1 = (bf16[128,1792]{1,0:T(8,128)(2,1)}, bf16[128,896]{1,0:T(8,128)(2,1)}, bf16[896,896]{1,0:T(8,128)(2,1)}) custom-call(bf16[1,128,1792]{2,1,0:T(8,128)(2,1)} %q_hbm.1, bf16[1,128,256]{2,1,0:T(8,128)(2,1)} %k_hbm.1, bf16[1,128,256]{2,1,0:T(8,128)(2,1)} %v_hbm.1, s32[1,128]{1,0:T(1,128)} %seg_hbm.1, s32[1,32]{1,0:T(1,128)} %start_hbm.1, ...), custom_call_target="tpu_custom_call" | custom-call | tf_op jit(solution)/shard_map/mega/pallas_call | solution.py:839
  100.0 3.7 %finish.1 = (bf16[1,128,1792]{2,1,0:T(8,128)(2,1)}, bf16[1,128,896]{2,1,0:T(8,128)(2,1)}, f32[296,896]{1,0:T(8,128)}, f32[296,896]{1,0:T(8,128)}, f32[296,896]{1,0:T(8,128)}) custom-call(bf16[128,1792]{1,0:T(8,128)(2,1)} %get-tuple-element.13.ctx_in, bf16[128,896]{1,0:T(8,128)(2,1)} %get-tuple-element.14.talker_in, bf16[896,896]{1,0:T(8,128)(2,1)} %get-tuple-element.15.grads_in), custom_call_target="tpu_custom_call" | custom-call | tf_op jit(solution)/shard_map/finish/pallas_call | solution.py:889

commit v8 on v7

--- a/solution.py
+++ b/solution.py
@@ -686,10 +686,11 @@
     ffn_in(-2)
     ffn_in(2)
     ffn_out(-2, 2)
+    ffn_in(-3)
+    ffn_in(3)
     net.settle()
     rows.ring(4, "ox")
-    ffn_in(-3)
-    ffn_in(3)
+    ffn_out(3, -3)
     ffn_in(4)
 
     b1 = HFirst(net, "b1", g32, res, 0, 32, b1_refs)
@@ -709,7 +710,7 @@
 
     grad(0, hid, gc)
     b1.start()
-    ffn_out(4, 3, -3)
+    ffn_out(4)
     grad(1, d_gate, gr)
     a1.start()
     swapped(4, 3, -3)

time: 104 us -> 104 us (level)
  no operation moved by 1% of the time
where the time goes in v8:
time: 104 us
  Pallas kernels  104 us (100%)
    pallas_call x1, Pallas kernels, fused(): pl.pallas_call(kernel, name='mega', out_shape=[jax.ShapeDtypeStruct((TOK,...  99.8 us
    pallas_call x1, Pallas kernels, finish(): pl.pallas_call(finish_kernel, name='finish', out_shape=[jax.ShapeDtypeStr...  3.68 us

profile of v8, /device:TPU:2, one launch (start us, length us, event | category | flops | bytes accessed | tf_op | source)
XLA Modules:
  0.0 104.3 jit_solution(4896465393009633017)
XLA Ops:
  0.6 99.8 %mega.1 = (bf16[128,1792]{1,0:T(8,128)(2,1)}, bf16[128,896]{1,0:T(8,128)(2,1)}, bf16[896,896]{1,0:T(8,128)(2,1)}) custom-call(bf16[1,128,1792]{2,1,0:T(8,128)(2,1)} %q_hbm.1, bf16[1,128,256]{2,1,0:T(8,128)(2,1)} %k_hbm.1, bf16[1,128,256]{2,1,0:T(8,128)(2,1)} %v_hbm.1, s32[1,128]{1,0:T(1,128)} %seg_hbm.1, s32[1,32]{1,0:T(1,128)} %start_hbm.1, ...), custom_call_target="tpu_custom_call" | custom-call | tf_op jit(solution)/shard_map/mega/pallas_call | solution.py:840
  100.5 3.7 %finish.1 = (bf16[1,128,1792]{2,1,0:T(8,128)(2,1)}, bf16[1,128,896]{2,1,0:T(8,128)(2,1)}, f32[296,896]{1,0:T(8,128)}, f32[296,896]{1,0:T(8,128)}, f32[296,896]{1,0:T(8,128)}) custom-call(bf16[128,1792]{1,0:T(8,128)(2,1)} %get-tuple-element.13.ctx_in, bf16[128,896]{1,0:T(8,128)(2,1)} %get-tuple-element.14.talker_in, bf16[896,896]{1,0:T(8,128)(2,1)} %get-tuple-element.15.grads_in), custom_call_target="tpu_custom_call" | custom-call | tf_op jit(solution)/shard_map/finish/pallas_call | solution.py:890
